TPU v7x, 32 devices: a whole 2x2x4 slice. The times are simulated.
32 devices in a mesh: dp: 16 (over z, y, x), tensor: 2 (over core).
Axes of the slice: x: 2, y: 2, z: 4, core: 2. Of those that a mesh axis runs over, the one named last changes fastest.
Arguments:
- tokens: bfloat16 [36864, 768], P(('dp', 'tensor')), may hold values from -6 to 6
- segment: int32 [36864], P('dp'), may hold values from -1 to 17, as said below
- norm_attn_gain: bfloat16 [768], P('dp'), may hold values from 0.099609375 to 1.8984375
- qkv_weight: bfloat16 [768, 3, 768], P('dp', None, 'tensor'), may hold values from -0.21875 to 0.21875
- attn_out_weight: bfloat16 [768, 768], P('tensor', 'dp'), may hold values from -0.625 to 0.625
- norm_mlp_gain: bfloat16 [768], P('dp'), may hold values from 0.099609375 to 1.8984375
- in_weight: bfloat16 [768, 2, 1152], P('dp', None, 'tensor'), may hold values from -0.21875 to 0.21875
- out_weight: bfloat16 [1152, 768], P('tensor', 'dp'), may hold values from -0.25 to 0.25
- cotangent: bfloat16 [36864, 768], P(('dp', 'tensor')), may hold values from -6 to 6
Outputs:
- layer_out: bfloat16 [36864, 768], P(('dp', 'tensor'))
- grad_tokens: float32 [36864, 768], P(('dp', 'tensor'))
- grad_norm_attn_gain: float32 [768], P('dp')
- grad_qkv_weight: float32 [768, 3, 768], P('dp', None, 'tensor')
- grad_attn_out_weight: float32 [768, 768], P('tensor', 'dp')
- grad_norm_mlp_gain: float32 [768], P('dp')
- grad_in_weight: float32 [768, 2, 1152], P('dp', None, 'tensor')
- grad_out_weight: float32 [1152, 768], P('tensor', 'dp')
Inputs may be any that keep to these rules, and one draw needn't show every extreme that they name: Within each group of 2304 slots, a sequence occupies whole consecutive padding blocks starting at the block named by its segment value; its live slots come first and fewer than 128 padding slots end its last block; whole padding blocks may end a group, at most a quarter of them. In every group one sequence holds the last slot of the first half of the group and the first slot of the second half.
All inputs are finite; a program needn't handle non-finite values.
Results may differ from a plain program's by a relative error of at most 0.018.
Values may be sent and summed in bfloat16 or wider, within the bound.
No kernel may reach another device: no remote copies, remote signals or barrier semaphores. Data moves between devices by JAX's collectives and lax.ppermute only.
A program may use at most 192 MiB of HBM per device.

v0:
```python
import jax
import jax.numpy as jnp
from jax import lax
from jax.sharding import PartitionSpec as P

HEAD_DIM = 64
WINDOW_HALF = 64
PAD_BLOCK = 128
QBLOCK = 1152


def passed_along(block, axis, distance):
    devices = range(lax.axis_size(axis))
    route = [(i - distance, i) for i in devices if i - distance in devices]
    return lax.ppermute(block, axis, route)


def layer_norm(values, gain):
    centred = values - jnp.mean(values, axis=-1, keepdims=True)
    spread = jnp.mean(centred * centred, axis=-1, keepdims=True)
    return centred * lax.rsqrt(spread + 1e-05) * gain


def rope_tables(position):
    half = HEAD_DIM // 2
    exponent = jnp.arange(half).astype(jnp.float32) * (2.0 / HEAD_DIM)
    inverse = jnp.power(10000.0, -exponent)
    angle = position.astype(jnp.float32)[:, None] * inverse[None, :]
    angle = jnp.concatenate([angle, angle], axis=-1)
    return (jnp.cos(angle)[:, None, :], jnp.sin(angle)[:, None, :])


def rotate(values, cosine, sine):
    half = values.shape[-1] // 2
    turned = jnp.concatenate([-values[..., half:], values[..., :half]], axis=-1)
    return values * cosine + turned * sine


def unrotate(values, cosine, sine):
    half = values.shape[-1] // 2
    scaled = values * sine
    return values * cosine + jnp.concatenate([scaled[..., half:], -scaled[..., :half]], axis=-1)


def split_windows(values):
    subs = QBLOCK // PAD_BLOCK
    lower = values[:QBLOCK].reshape((subs, PAD_BLOCK) + values.shape[1:])
    upper = values[PAD_BLOCK:].reshape((subs, PAD_BLOCK) + values.shape[1:])
    return jnp.concatenate([lower, upper], axis=1)


def merge_windows(values):
    rest = values.shape[2:]
    lower = values[:, :PAD_BLOCK].reshape((QBLOCK,) + rest)
    upper = values[:, PAD_BLOCK:].reshape((QBLOCK,) + rest)
    margin = ((0, 0),) * len(rest)
    return jnp.pad(lower, ((0, PAD_BLOCK),) + margin) + jnp.pad(upper, ((PAD_BLOCK, 0),) + margin)


def windows(queries, key_pad, value_pad, seg_query, seg_pad):
    subs = QBLOCK // PAD_BLOCK
    query_blk = queries.reshape((subs, PAD_BLOCK) + queries.shape[1:])
    key_sub = split_windows(key_pad)
    value_sub = split_windows(value_pad)
    seg_rows = seg_query.reshape(subs, PAD_BLOCK)
    seg_cols = split_windows(seg_pad)
    raw = jnp.einsum("sqhd,skhd->hsqk", query_blk, key_sub, preferred_element_type=jnp.float32)
    row_pos = jnp.arange(PAD_BLOCK, dtype=jnp.int32)[:, None]
    col_pos = jnp.arange(PAD_BLOCK + 2 * WINDOW_HALF, dtype=jnp.int32)[None, :] - WINDOW_HALF
    band = jnp.abs(row_pos - col_pos) <= WINDOW_HALF
    allowed = (seg_rows[:, :, None] == seg_cols[:, None, :]) & band[None]
    scores = jnp.where(allowed[None], raw * HEAD_DIM ** (-0.5), -1e30)
    return (query_blk, key_sub, value_sub, scores)


def attend_forward(queries, key_pad, value_pad, seg_query, seg_pad):

    def one_block(carry, start):
        query_blk, key_sub, value_sub, scores = windows(
            queries, key_pad, value_pad, seg_query, seg_pad
        )
        top = jnp.max(scores, axis=-1, keepdims=True)
        weights = jnp.exp(scores - top)
        total = jnp.sum(weights, axis=-1, keepdims=True)
        probs_low = (weights / total).astype(jnp.bfloat16)
        out_blk = jnp.einsum(
            "hsqk,skhd->sqhd", probs_low, value_sub, preferred_element_type=jnp.float32
        )
        return (
            carry,
            (out_blk.reshape((QBLOCK,) + queries.shape[1:]), (top + jnp.log(total))[..., 0]),
        )

    starts = jnp.arange(queries.shape[0] // QBLOCK, dtype=jnp.int32) * QBLOCK
    unused, (outputs, logsum) = lax.scan(one_block, None, starts)
    return (outputs.reshape(queries.shape), logsum)


def attend_backward(queries, key_pad, value_pad, grad_attended, logsum, seg_query, seg_pad):
    subs = QBLOCK // PAD_BLOCK

    def one_block(carry, item):
        start, logsum_blk = item
        key_acc, value_acc = carry
        query_blk, key_sub, value_sub, scores = windows(
            queries, key_pad, value_pad, seg_query, seg_pad
        )
        probs = jnp.exp(scores - logsum_blk[..., None])
        probs_low = probs.astype(jnp.bfloat16)
        grad_blk = grad_attended.reshape((subs, PAD_BLOCK) + queries.shape[1:])
        grad_probs = jnp.einsum(
            "sqhd,skhd->hsqk", grad_blk, value_sub, preferred_element_type=jnp.float32
        )
        delta = jnp.sum(grad_probs * probs, axis=-1, keepdims=True)
        grad_scores = (probs * (grad_probs - delta)).astype(jnp.bfloat16)
        scale = HEAD_DIM ** (-0.5)
        grad_query = (
            jnp.einsum("hsqk,skhd->sqhd", grad_scores, key_sub, preferred_element_type=jnp.float32)
            * scale
        )
        grad_key_sub = (
            jnp.einsum(
                "hsqk,sqhd->skhd", grad_scores, query_blk, preferred_element_type=jnp.float32
            )
            * scale
        )
        grad_value_sub = jnp.einsum(
            "hsqk,sqhd->skhd", probs_low, grad_blk, preferred_element_type=jnp.float32
        )
        key_acc = key_acc + merge_windows(grad_key_sub)
        value_acc = value_acc + merge_windows(grad_value_sub)
        return ((key_acc, value_acc), grad_query.reshape((QBLOCK,) + queries.shape[1:]))

    starts = jnp.arange(queries.shape[0] // QBLOCK, dtype=jnp.int32) * QBLOCK
    init = (jnp.zeros(key_pad.shape, jnp.float32), jnp.zeros(key_pad.shape, jnp.float32))
    (key_acc, value_acc), grad_queries = lax.scan(one_block, init, (starts, logsum))
    return (grad_queries.reshape(queries.shape), key_acc, value_acc)


def gelu_gate(pre_act):
    return jax.nn.gelu(pre_act[:, 0], approximate=False) * pre_act[:, 1]


def neighbour(piece, by):
    return passed_along(piece.astype(jnp.bfloat16), "tensor", by).astype(piece.dtype)


def body(
    tokens,
    segment,
    norm_attn_gain,
    qkv_weight,
    attn_out_weight,
    norm_mlp_gain,
    in_weight,
    out_weight,
    cotangent,
):
    local_rows = tokens.shape[0]
    index = lax.axis_index("tensor")
    gain_one, weight_qkv, weight_attn, gain_two, weight_in, weight_out = (
        lax.all_gather(norm_attn_gain, "dp", axis=0, tiled=True),
        lax.all_gather(qkv_weight, "dp", axis=0, tiled=True),
        lax.all_gather(attn_out_weight, "dp", axis=1, tiled=True),
        lax.all_gather(norm_mlp_gain, "dp", axis=0, tiled=True),
        lax.all_gather(in_weight, "dp", axis=0, tiled=True),
        lax.all_gather(out_weight, "dp", axis=1, tiled=True),
    )
    inputs = tokens.astype(jnp.float32)
    own_segment = lax.dynamic_slice_in_dim(segment, index * local_rows, local_rows, 0)
    normed, norm_one_pull = jax.vjp(layer_norm, inputs, gain_one.astype(jnp.float32))
    normed_low = normed.astype(jnp.bfloat16)
    weight_qkv, weight_attn, weight_in, weight_out = (
        lax.all_gather(weight_qkv, "tensor", axis=2, tiled=True),
        lax.all_gather(weight_attn, "tensor", axis=0, tiled=True),
        lax.all_gather(weight_in, "tensor", axis=2, tiled=True),
        lax.all_gather(weight_out, "tensor", axis=0, tiled=True),
    )
    first_slot = index * local_rows
    row_count = normed_low.shape[0]
    local_width = weight_qkv.shape[2]
    heads_here = local_width // HEAD_DIM
    shape = (row_count, heads_here, HEAD_DIM)
    projected = jnp.einsum(
        "rd,dcf->rcf", normed_low, weight_qkv, preferred_element_type=jnp.float32
    )
    slots = first_slot + jnp.arange(row_count, dtype=jnp.int32)
    position = jnp.where(own_segment >= 0, slots - PAD_BLOCK * own_segment, 0)
    cosine, sine = rope_tables(position)
    queries = rotate(projected[:, 0].reshape(shape), cosine, sine).astype(jnp.bfloat16)
    keys_rot = rotate(projected[:, 1].reshape(shape), cosine, sine).astype(jnp.bfloat16)
    value_rows = projected[:, 2].reshape(shape).astype(jnp.bfloat16)
    seg_pad_full = jnp.pad(segment, (WINDOW_HALF, WINDOW_HALF), constant_values=-2)
    paired = jnp.stack([keys_rot, value_rows], axis=1).astype(jnp.float32)
    from_below = neighbour(paired[row_count - WINDOW_HALF :], 1)
    from_above = neighbour(paired[:WINDOW_HALF], -1)
    extended = jnp.concatenate([from_below, paired, from_above], axis=0).astype(jnp.bfloat16)
    key_pad = extended[:, 0]
    value_pad = extended[:, 1]
    seg_pad = lax.dynamic_slice_in_dim(
        seg_pad_full, index * local_rows, local_rows + 2 * WINDOW_HALF, 0
    )
    attended, logsum = attend_forward(queries, key_pad, value_pad, own_segment, seg_pad)
    attended_low = attended.reshape(row_count, local_width).astype(jnp.bfloat16)
    hidden = inputs + jnp.dot(attended_low, weight_attn, preferred_element_type=jnp.float32)
    normed_two, norm_two_pull = jax.vjp(layer_norm, hidden, gain_two.astype(jnp.float32))
    normed_two_low = normed_two.astype(jnp.bfloat16)
    pre_act = jnp.einsum(
        "rd,dcf->rcf", normed_two_low, weight_in, preferred_element_type=jnp.float32
    )
    gated, gate_pull = jax.vjp(gelu_gate, pre_act)
    gated_low = gated.astype(jnp.bfloat16)
    layer_out = (
        hidden + jnp.dot(gated_low, weight_out, preferred_element_type=jnp.float32)
    ).astype(jnp.bfloat16)
    grad_y = cotangent.astype(jnp.float32) * (own_segment >= 0).astype(jnp.float32)[:, None]
    grad_y_rows = grad_y.astype(jnp.bfloat16)
    grad_weight_out = jnp.einsum(
        "rf,rd->fd", gated_low, grad_y_rows, preferred_element_type=jnp.float32
    )
    grad_gated = jnp.einsum(
        "rd,fd->rf", grad_y_rows, weight_out, preferred_element_type=jnp.float32
    )
    grad_pre = gate_pull(grad_gated)[0].astype(jnp.bfloat16)
    grad_weight_in = jnp.einsum(
        "rd,rcf->dcf", normed_two_low, grad_pre, preferred_element_type=jnp.float32
    )
    grad_normed_two = jnp.einsum(
        "rcf,dcf->rd", grad_pre, weight_in, preferred_element_type=jnp.float32
    )
    grad_hidden_norm, grad_gain_two = norm_two_pull(grad_normed_two)
    grad_hidden = grad_y + grad_hidden_norm
    grad_hidden_rows = grad_hidden.astype(jnp.bfloat16)
    grad_weight_attn = jnp.einsum(
        "rf,rd->fd", attended_low, grad_hidden_rows, preferred_element_type=jnp.float32
    )
    grad_attended = jnp.einsum(
        "rd,fd->rf", grad_hidden_rows, weight_attn, preferred_element_type=jnp.float32
    ).astype(jnp.bfloat16)
    grad_queries, key_acc, value_acc = attend_backward(
        queries, key_pad, value_pad, grad_attended.reshape(shape), logsum, own_segment, seg_pad
    )
    paired_grad = jnp.stack([key_acc, value_acc], axis=1)
    from_lower = neighbour(paired_grad[row_count + WINDOW_HALF :], 1)
    from_upper = neighbour(paired_grad[:WINDOW_HALF], -1)
    rest = ((0, 0), (0, 0), (0, 0))
    core = paired_grad[WINDOW_HALF : WINDOW_HALF + row_count]
    core = (
        core
        + jnp.pad(from_lower, ((0, row_count - WINDOW_HALF),) + rest)
        + jnp.pad(from_upper, ((row_count - WINDOW_HALF, 0),) + rest)
    )
    grad_keys = core[:, 0]
    grad_values = core[:, 1]
    grad_queries = unrotate(grad_queries, cosine, sine).reshape(row_count, local_width)
    grad_keys = unrotate(grad_keys, cosine, sine).reshape(row_count, local_width)
    grad_qkv = jnp.stack(
        [grad_queries, grad_keys, grad_values.reshape(row_count, local_width)], axis=1
    ).astype(jnp.bfloat16)
    grad_weight_qkv = jnp.einsum(
        "rd,rcf->dcf", normed_low, grad_qkv, preferred_element_type=jnp.float32
    )
    grad_normed = jnp.einsum(
        "rcf,dcf->rd", grad_qkv, weight_qkv, preferred_element_type=jnp.float32
    )
    grad_input_norm, grad_gain_one = norm_one_pull(grad_normed)
    grad_tokens = grad_hidden + grad_input_norm
    grad_gain_one, grad_gain_two = lax.psum((grad_gain_one, grad_gain_two), "tensor")
    owned_gain_one, owned_qkv, owned_attn, owned_gain_two, owned_in, owned_out = (
        lax.psum_scatter(grad_gain_one, "dp", scatter_dimension=0, tiled=True),
        lax.psum_scatter(grad_weight_qkv, "dp", scatter_dimension=0, tiled=True),
        lax.psum_scatter(grad_weight_attn, "dp", scatter_dimension=1, tiled=True),
        lax.psum_scatter(grad_gain_two, "dp", scatter_dimension=0, tiled=True),
        lax.psum_scatter(grad_weight_in, "dp", scatter_dimension=0, tiled=True),
        lax.psum_scatter(grad_weight_out, "dp", scatter_dimension=1, tiled=True),
    )
    owned_qkv, owned_attn, owned_in, owned_out = (
        lax.psum_scatter(
            owned_qkv.astype(jnp.bfloat16), "tensor", scatter_dimension=2, tiled=True
        ).astype(jnp.float32),
        lax.psum_scatter(
            owned_attn.astype(jnp.bfloat16), "tensor", scatter_dimension=0, tiled=True
        ).astype(jnp.float32),
        lax.psum_scatter(
            owned_in.astype(jnp.bfloat16), "tensor", scatter_dimension=2, tiled=True
        ).astype(jnp.float32),
        lax.psum_scatter(
            owned_out.astype(jnp.bfloat16), "tensor", scatter_dimension=0, tiled=True
        ).astype(jnp.float32),
    )
    return (
        layer_out,
        grad_tokens,
        owned_gain_one,
        owned_qkv,
        owned_attn,
        owned_gain_two,
        owned_in,
        owned_out,
    )


def solution(mesh):
    placed = (
        P(("dp", "tensor"), None),
        P("dp"),
        P("dp"),
        P("dp", None, "tensor"),
        P("tensor", "dp"),
        P("dp"),
        P("dp", None, "tensor"),
        P("tensor", "dp"),
        P(("dp", "tensor"), None),
    )
    return jax.shard_map(
        body,
        mesh=mesh,
        in_specs=placed,
        out_specs=(
            P(("dp", "tensor"), None),
            P(("dp", "tensor"), None),
            P("dp"),
            P("dp", None, "tensor"),
            P("tensor", "dp"),
            P("dp"),
            P("dp", None, "tensor"),
            P("tensor", "dp"),
        ),
        check_vma=False,
    )
```

profile of v0, /device:TPU:0, one launch (start us, length us, event | category | flops | bytes accessed | tf_op | source)
XLA Modules:
  0.0 1008.5 jit_solution(17719507913655826954)
XLA Ops:
  7.9 49.8 %all_gather.38 = bf16[576,768]{0,1:T(8,128)(2,1)S(1)} all-gather(bf16[576,48]{0,1:T(8,128)(2,1)} %param.16), channel_id=1, replica_groups=mesh['dp'=16,'tensor'=2] {'dp'}, dimensions={1}, use_global_device_ids=true | all-gather | bytes 940032 | tf_op jit(solution)/shard_map/all_gather | solution.py:167
  59.8 15.1 %all-gather.7.cloned.1.call-done = bf16[768,3,384]{2,0,1:T(8,128)(2,1)} async-done(((bf16[48,3,384]{2,0,1:T(8,128)(2,1)}), bf16[768,3,384]{2,0,1:T(8,128)(2,1)}) %all-gather.7.cloned.1.call-update) | async-done | bytes 1769488 | tf_op jit(solution)/shard_map/all_gather | solution.py:163
  78.8 44.9 %all_gather.33 = bf16[384,768]{0,1:T(8,128)(2,1)} all-gather(bf16[384,48]{0,1:T(8,128)(2,1)S(1)} %copy-done.46), channel_id=1, replica_groups=mesh['dp'=16,'tensor'=2] {'dp'}, dimensions={1}, use_global_device_ids=true | all-gather | bytes 626688 | tf_op jit(solution)/shard_map/all_gather | solution.py:164
  132.3 36.9 %all-reduce.15 = (bf16[768]{0:T(1024)(128)(2,1)S(1)}, bf16[768]{0:T(1024)(128)(2,1)S(1)}) all-reduce(bf16[768]{0:T(1024)(128)(2,1)S(1)} %dynamic-update-slice, bf16[768]{0:T(1024)(128)(2,1)S(1)} %dynamic-update-slice.1), channel_id=1, replica_groups=mesh['dp'=16,'tensor'=2] {'dp'}, use_global_device_ids=true, to_apply=%add.9 | all-reduce | flops 1536 | bytes 6144
  192.7 7.3 fusion.85
  232.1 7.4 pad_maximum_fusion.6
  256.4 7.2 fusion.111
  268.5 8.0 fusion.5
  290.1 6.9 convert_bitcast_fusion
  306.4 7.7 fusion.101
  314.2 13.0 %multiply_bitcast_fusion.1 = (f32[1152,1,1152]{2,0,1:T(8,128)S(1)}, f32[1152,1152]{1,0:T(8,128)S(1)}) fusion(f32[1152,1152]{1,0:T(8,128)} %fusion.79, f32[1152,2,1152]{2,0,1:T(8,128)S(1)} %fusion.101), kind=kLoop, calls=%fused_computation.50 | loop fusion | flops 86261760 | bytes 21233664 | tf_op jit(solution)/shard_map/transpose(jvp())/broadcast_in_dim | solution.py:141
  327.2 8.4 fusion.28
  335.6 10.1 %multiply_reduce_fusion.1 = (f32[768]{0:T(1024)}, f32[1152]{0:T(1024)S(1)}, f32[1152,768]{0,1:T(8,128)S(1)}) fusion(f32[1152,768]{0,1:T(8,128)S(1)} %copy-done.16, f32[1152]{0:T(1024)S(1)} %fusion.95, f32[1152]{0:T(1024)S(1)} %broadcast_multiply_fusion.2, f32[768]{0:T(1024)S(1)} %copy-done.50, bf16[768,2,1152]{0,2,1:T(8,128)(2,1)} %all-gather.15.cloned.1.call-done, ...), kind=kOutput, calls=%fused_computation.104 | convolution fusion | flops 4088363008 | bytes 21253632 | tf_op jit(solution)/shard_map/rcf,dcf->rd/dot_general | solution.py:228
  373.7 14.1 %fusion.83 = f32[768,2,1152]{2,0,1:T(8,128)} fusion(f32[1152,1,1152]{2,0,1:T(8,128)} %get-tuple-element.113, f32[1152,1,1152]{2,0,1:T(8,128)} %copy-done.21, f32[1152,768]{0,1:T(8,128)} %copy-done.15, f32[768]{0:T(1024)S(1)} %copy-done.51, f32[1152]{0:T(1024)S(1)} %copy-done.49, f32[1152]{0:T(1024)S(1)} %copy-done.41), kind=kOutput, calls=%fused_computation.152 | convolution fusion | flops 4085710848 | bytes 21245952 | tf_op jit(solution)/shard_map/rd,rcf->dcf/dot_general | solution.py:225
  396.9 7.2 fusion.54
  404.1 92.1 %multiply_convert_fusion = bf16[12,9,128,256]{3,2,1,0:T(8,128)(2,1)} fusion(f32[12,9,128,256]{3,2,1,0:T(8,128)} %fusion.54, f32[12,9,128,256]{3,2,1,0:T(8,128)} %copy-done, f32[12,9,128]{2,1,0:T(8,128)S(1)} %copy-done.33), kind=kOutput, calls=%fused_computation.1 | output fusion | flops 21247744 | bytes 35444736 | tf_op jit(solution)/shard_map/while/body/eval_jaxpr/sub | solution.py:115
  524.8 7.8 reshape.440
  564.6 7.5 add_convert_fusion.2
  581.6 7.5 fusion.57
  596.3 10.5 %fusion.50 = (f32[1152]{0:T(1024)}, f32[1152,768]{0,1:T(8,128)}) fusion(bf16[1152,768]{0,1:T(8,128)(2,1)S(1)} %copy-done.2, f32[768]{0:T(1024)} %convert_element_type.144, f32[1152]{0:T(1024)S(1)} %copy-done.35, bf16[768,3,768]{0,2,1:T(8,128)(2,1)} %all-gather.9.cloned.1.call-done, bf16[1152,1,768]{2,0,1:T(8,128)(2,1)S(1)} %copy.157, ...), kind=kOutput, calls=%fused_computation.83 | convolution fusion | flops 4086594560 | bytes 14168064 | tf_op jit(solution)/shard_map/rcf,dcf->rd/dot_general | solution.py:263
  606.8 13.9 %reduce-scatter.23.cloned.1.call-done = f32[1152,48]{0,1:T(8,128)} async-done(((f32[1152,768]{0,1:T(8,128)}), f32[1152,48]{0,1:T(8,128)}) %reduce-scatter.23.cloned.1.call-update) | async-done | bytes 221200 | tf_op jit(solution)/shard_map/reduce_scatter | solution.py:275
  623.9 153.4 %reduce-scatter.21.cloned.1.call-done = f32[48,2,1152]{2,0,1:T(8,128)} async-done(((f32[768,2,1152]{2,0,1:T(8,128)}), f32[48,2,1152]{2,0,1:T(8,128)}) %reduce-scatter.21.cloned.1.call-update) | async-done | bytes 442384 | tf_op jit(solution)/shard_map/reduce_scatter | solution.py:274
  785.2 148.3 %reduce-scatter.17.cloned.1.call-done = f32[48,3,768]{2,0,1:T(8,128)} async-done(((f32[768,3,768]{2,0,1:T(8,128)}), f32[48,3,768]{2,0,1:T(8,128)}) %reduce-scatter.17.cloned.1.call-update) | async-done | bytes 442384 | tf_op jit(solution)/shard_map/reduce_scatter | solution.py:271
  946.1 40.0 %all-reduce.13 = (f32[768]{0:T(1024)S(1)}, f32[768]{0:T(1024)S(1)}) all-reduce(f32[768]{0:T(1024)} %get-tuple-element.99, f32[768]{0:T(1024)} %get-tuple-element.97), channel_id=2, replica_groups=mesh['dp'=16,'tensor'=2] {'dp'}, use_global_device_ids=true, to_apply=%region_13.14.clone | all-reduce | flops 1536 | bytes 12288
  (289 shorter events, 267.1 us)
Async XLA Ops:
  7.2 67.8 %all-gather.7.cloned.1.call-start = ((), (), s32[]{:S(2)}) async-start(), calls=%async_computation.8 | async-start | bytes 1880064 | tf_op jit(solution)/shard_map/all_gather | solution.py:163
  7.9 171.2 %all-gather.17.cloned.1.call-start = ((), (), s32[]{:S(2)}) async-start(), calls=%async_computation.13 | async-start | bytes 2654208 | tf_op jit(solution)/shard_map/all_gather | solution.py:177
  59.1 126.4 %all-gather.13.cloned.1.call-start = ((), (), s32[]{:S(2)}) async-start(), calls=%async_computation.11 | async-start | bytes 2088960 | tf_op jit(solution)/shard_map/all_gather | solution.py:166
  59.8 132.9 %all-gather.9.cloned.1.call-start = ((), (), s32[]{:S(2)}) async-start(), calls=%async_computation.9 | async-start | bytes 5308416 | tf_op jit(solution)/shard_map/all_gather | solution.py:174
  78.8 221.4 %all-gather.11.cloned.1.call-start = ((), (), s32[]{:S(2)}) async-start(), calls=%async_computation.10 | async-start | bytes 1769472 | tf_op jit(solution)/shard_map/all_gather | solution.py:175
  123.7 182.7 %all-gather.15.cloned.1.call-start = ((), (), s32[]{:S(2)}) async-start(), calls=%async_computation.12 | async-start | bytes 5308416 | tf_op jit(solution)/shard_map/all_gather | solution.py:176
  124.5 229.4 %copy-start.36 = (f32[1152]{0:T(1024)}, f32[1152]{0:T(1024)S(1)}, u32[]{:S(2)}) copy-start(f32[1152]{0:T(1024)S(1)} %get-tuple-element.111) | copy-start | bytes 13828
  129.1 171.1 %copy-start.1 = (bf16[1152,768]{0,1:T(8,128)(2,1)}, bf16[1152,768]{0,1:T(8,128)(2,1)S(1)}, u32[]{:S(2)}) copy-start(bf16[1152,768]{0,1:T(8,128)(2,1)S(1)} %copy.121) | copy-start | bytes 5308420
  173.9 179.9 %copy-start.12 = (bf16[1152,768]{0,1:T(8,128)(2,1)}, bf16[1152,768]{0,1:T(8,128)(2,1)S(1)}, u32[]{:S(2)}) copy-start(bf16[1152,768]{0,1:T(8,128)(2,1)S(1)} %copy.135) | copy-start | bytes 5308420
  192.1 400.8 %reduce-scatter.19.cloned.1.call-start = ((), (), s32[]{:S(2)}) async-start(), calls=%async_computation.15 | async-start | bytes 2506752 | tf_op jit(solution)/shard_map/reduce_scatter | solution.py:272
  226.6 5.4 collective-permute-start
  228.2 3.9 collective-permute-start.1
  353.6 267.0 %reduce-scatter.23.cloned.1.call-start = ((), (), s32[]{:S(2)}) async-start(), calls=%async_computation.17 | async-start | bytes 3760128 | tf_op jit(solution)/shard_map/reduce_scatter | solution.py:275
  360.2 417.2 %reduce-scatter.21.cloned.1.call-start = ((), (), s32[]{:S(2)}) async-start(), calls=%async_computation.16 | async-start | bytes 7520256 | tf_op jit(solution)/shard_map/reduce_scatter | solution.py:274
  387.9 545.5 %reduce-scatter.17.cloned.1.call-start = ((), (), s32[]{:S(2)}) async-start(), calls=%async_computation.14 | async-start | bytes 7520256 | tf_op jit(solution)/shard_map/reduce_scatter | solution.py:271
  396.9 106.6 %copy-start.4 = (f32[1280,1,12,64]{0,3,2,1:T(8,128)}, f32[1280,1,12,64]{0,3,2,1:T(8,128)S(1)}, u32[]{:S(2)}) copy-start(f32[1280,1,12,64]{0,3,2,1:T(8,128)S(1)} %add_bitcast_fusion) | copy-start | bytes 11796484
  506.6 26.0 %collective-permute-start.2 = (bf16[64,2,12,64]{0,3,2,1:T(8,128)(2,1)}, bf16[64,2,12,64]{0,3,2,1:T(8,128)(2,1)}, u32[]{:S(2)}, u32[]{:S(2)}) collective-permute-start(bf16[64,2,12,64]{0,3,2,1:T(8,128)(2,1)} %get-tuple-element.123), channel_id=1, source_target_pairs={{0,1},{2,3},{4,5},{6,7},{8,9},{10,11},{12,13},{14,15},{16,17},{18,... | collective-permute-start | bytes 589832 | tf_op jit(solution)/shard_map/ppermute | solution.py:15
  510.7 21.9 %collective-permute-start.3 = (bf16[64,2,12,64]{0,3,2,1:T(8,128)(2,1)}, bf16[64,2,12,64]{0,3,2,1:T(8,128)(2,1)}, u32[]{:S(2)}, u32[]{:S(2)}) collective-permute-start(bf16[64,2,12,64]{0,3,2,1:T(8,128)(2,1)} %get-tuple-element.124), channel_id=1, source_target_pairs={{1,0},{3,2},{5,4},{7,6},{9,8},{11,10},{13,12},{15,14},{17,16},{19,... | collective-permute-start | bytes 589832 | tf_op jit(solution)/shard_map/ppermute | solution.py:15
  580.7 413.6 %reduce-scatter.27.cloned.1.call-start = ((), (), s32[]{:S(2)}) async-start(), calls=%async_computation.19 | async-start | bytes 294912
  596.2 399.7 %reduce-scatter.31.cloned.1.call-start = ((), (), s32[]{:S(2)}) async-start(), calls=%async_computation.21 | async-start | bytes 442368
  622.5 375.1 %reduce-scatter.29.cloned.1.call-start = ((), (), s32[]{:S(2)}) async-start(), calls=%async_computation.20 | async-start | bytes 442368
  780.1 219.5 %reduce-scatter.25.cloned.1.call-start = ((), (), s32[]{:S(2)}) async-start(), calls=%async_computation.18 | async-start | bytes 589824
  780.4 159.1 %copy-start.13 = (bf16[1152,768]{0,1:T(8,128)(2,1)S(1)}, bf16[1152,768]{0,1:T(8,128)(2,1)}, u32[]{:S(2)}) copy-start(bf16[1152,768]{0,1:T(8,128)(2,1)} %copy-done.12) | copy-start | bytes 5308420
  780.4 159.1 %copy-start.37 = (f32[1152]{0:T(1024)S(1)}, f32[1152]{0:T(1024)}, u32[]{:S(2)}) copy-start(f32[1152]{0:T(1024)} %copy-done.36) | copy-start | bytes 13828
  (56 other events, 635.8 us)
Sparse Core Ops, SparseCore 0:
  10.7 64.1 all-gather.6
  77.0 8.8 all-gather.16
  88.7 61.5 all-gather.12
  152.3 11.3 all-gather.8
  165.1 10.3 all-gather.10
  192.2 10.2 all-gather.14
  353.7 127.6 reduce-scatter.18
  487.3 133.2 reduce-scatter.22
  626.9 150.4 reduce-scatter.20
  783.4 149.9 reduce-scatter.16
  936.3 6.3 reduce-scatter.26
  944.9 8.8 reduce-scatter.30
  956.1 8.8 reduce-scatter.28
  967.1 8.9 reduce-scatter.24
where the time goes:
time: 1020 us; the launch traced here: 1010 us
  waiting for transfers between devices  332 us (33%)
  other arithmetic  199 us (20%)
  blocking collectives  175 us (17%)
  local copies, waits for them, and re-layouts  151 us (15%)
  matrix products  124 us (12%)
  between operations  16.5 us (2%)
  starting transfers between devices  10.5 us (1%)
    reduce_scatter x1, waiting for transfers between devices, body(): lax.psum_scatter(grad_weight_in, 'dp', scatter_dimension=0, tiled=True)  153 us
    reduce_scatter x1, waiting for transfers between devices, body(): lax.psum_scatter(grad_weight_qkv, 'dp', scatter_dimension=0, tiled=True)  148 us
    sub x1, other arithmetic, one_block(): grad_scores = (probs * (grad_probs - delta)).astype(jnp.bfloat16)  92.1 us
    unnamed x2, blocking collectives  76.9 us
    unnamed x150, local copies, waits for them, and re-layouts  52 us
    all_gather x1, blocking collectives, body(): lax.all_gather(out_weight, 'dp', axis=1, tiled=True)  49.8 us
    all_gather x1, blocking collectives, body(): lax.all_gather(attn_out_weight, 'dp', axis=1, tiled=True)  44.9 us
    broadcast_in_dim x2, other arithmetic, gelu_gate(): return jax.nn.gelu(pre_act[:, 0], approximate=False) * pre_act[:, 1]  21.4 us
  transfers between devices with their start and end apart: 18, of which 4 were waited for; matrix products, arithmetic and copies ran while one was open for 41% of the time, Pallas kernels for 0%

commit v1 on v0

--- a/solution.py
+++ b/solution.py
@@ -145,6 +145,66 @@
     return passed_along(piece.astype(jnp.bfloat16), "tensor", by).astype(piece.dtype)
 
 
+def steps_of(devices, swapped):
+    bits = [1 << i for i in range(devices.bit_length() - 1)]
+    near, far = bits[:2], bits[2:]
+    return far + (near if swapped else near[::-1])
+
+
+def exchanged(block, mask):
+    devices = lax.axis_size("dp")
+    return lax.ppermute(block, "dp", [(i, i ^ mask) for i in range(devices)])
+
+
+def swapped_cores(block):
+    return lax.ppermute(block, "tensor", [(0, 1), (1, 0)])
+
+
+def gather_rows(shard, swapped):
+    devices = lax.axis_size("dp")
+    index = lax.axis_index("dp")
+    levels = devices.bit_length() - 1
+    held = shard.reshape((1,) * levels + shard.shape)
+    for mask in steps_of(devices, swapped):
+        axis = levels - mask.bit_length()
+        other = exchanged(held, mask)
+        held = jnp.where(
+            (index & mask) == 0,
+            jnp.concatenate([held, other], axis=axis),
+            jnp.concatenate([other, held], axis=axis),
+        )
+    return held.reshape(devices * shard.shape[0], shard.shape[1])
+
+
+def scatter_rows(total, swapped):
+    devices = lax.axis_size("dp")
+    index = lax.axis_index("dp")
+    levels = devices.bit_length() - 1
+    rows = total.shape[0] // devices
+    held = total.reshape((2,) * levels + (rows, total.shape[1]))
+    for mask in reversed(steps_of(devices, swapped)):
+        axis = levels - mask.bit_length()
+        bit = (index & mask) // mask
+        keep = lax.dynamic_slice_in_dim(held, bit, 1, axis)
+        send = lax.dynamic_slice_in_dim(held, 1 - bit, 1, axis)
+        other = exchanged(send.astype(jnp.bfloat16), mask)
+        held = keep.astype(jnp.float32) + other.astype(jnp.float32)
+    return held.reshape(rows, total.shape[1])
+
+
+def both_halves(own):
+    other = swapped_cores(own)
+    first = lax.axis_index("tensor") == 0
+    return jnp.where(first, jnp.stack([own, other]), jnp.stack([other, own]))
+
+
+def own_half(both):
+    index = lax.axis_index("tensor")
+    keep = lax.dynamic_index_in_dim(both, index, 0, keepdims=False)
+    send = lax.dynamic_index_in_dim(both, 1 - index, 0, keepdims=False)
+    return keep.astype(jnp.float32) + swapped_cores(send.astype(jnp.bfloat16)).astype(jnp.float32)
+
+
 def body(
     tokens,
     segment,
@@ -158,24 +218,33 @@
 ):
     local_rows = tokens.shape[0]
     index = lax.axis_index("tensor")
-    gain_one, weight_qkv, weight_attn, gain_two, weight_in, weight_out = (
-        lax.all_gather(norm_attn_gain, "dp", axis=0, tiled=True),
-        lax.all_gather(qkv_weight, "dp", axis=0, tiled=True),
-        lax.all_gather(attn_out_weight, "dp", axis=1, tiled=True),
-        lax.all_gather(norm_mlp_gain, "dp", axis=0, tiled=True),
-        lax.all_gather(in_weight, "dp", axis=0, tiled=True),
-        lax.all_gather(out_weight, "dp", axis=1, tiled=True),
-    )
+    own_rows = norm_attn_gain.shape[0]
+    half_width = qkv_weight.shape[2]
+    half_units = in_weight.shape[2]
+    gains = jnp.pad(jnp.stack([norm_attn_gain, norm_mlp_gain], axis=1), ((0, 0), (0, 126)))
+    query_key = gather_rows(qkv_weight[:, :2].reshape(own_rows, -1), False)
+    value_gain = gather_rows(jnp.concatenate([qkv_weight[:, 2], gains], axis=1), True)
+    up = gather_rows(in_weight.reshape(own_rows, -1), False)
+    down = gather_rows(jnp.concatenate([attn_out_weight.T, out_weight.T], axis=1), True)
+    width = query_key.shape[0]
+    gain_one = value_gain[:, half_width]
+    gain_two = value_gain[:, half_width + 1]
+    query_key = both_halves(query_key)
+    value_half = both_halves(value_gain[:, :half_width])
+    up = both_halves(up)
+    down = both_halves(down)
+    weight_qkv = jnp.concatenate(
+        [query_key.reshape(2, width, 2, half_width), value_half[:, :, None]], axis=2
+    ).transpose(1, 2, 0, 3).reshape(width, 3, 2 * half_width)
+    weight_in = up.reshape(2, width, 2, half_units).transpose(1, 2, 0, 3).reshape(
+        width, 2, 2 * half_units
+    )
+    weight_attn = down[:, :, :half_width].transpose(0, 2, 1).reshape(2 * half_width, width)
+    weight_out = down[:, :, half_width:].transpose(0, 2, 1).reshape(2 * half_units, width)
     inputs = tokens.astype(jnp.float32)
     own_segment = lax.dynamic_slice_in_dim(segment, index * local_rows, local_rows, 0)
     normed, norm_one_pull = jax.vjp(layer_norm, inputs, gain_one.astype(jnp.float32))
     normed_low = normed.astype(jnp.bfloat16)
-    weight_qkv, weight_attn, weight_in, weight_out = (
-        lax.all_gather(weight_qkv, "tensor", axis=2, tiled=True),
-        lax.all_gather(weight_attn, "tensor", axis=0, tiled=True),
-        lax.all_gather(weight_in, "tensor", axis=2, tiled=True),
-        lax.all_gather(weight_out, "tensor", axis=0, tiled=True),
-    )
     first_slot = index * local_rows
     row_count = normed_low.shape[0]
     local_width = weight_qkv.shape[2]
@@ -265,29 +334,37 @@
     )
     grad_input_norm, grad_gain_one = norm_one_pull(grad_normed)
     grad_tokens = grad_hidden + grad_input_norm
-    grad_gain_one, grad_gain_two = lax.psum((grad_gain_one, grad_gain_two), "tensor")
-    owned_gain_one, owned_qkv, owned_attn, owned_gain_two, owned_in, owned_out = (
-        lax.psum_scatter(grad_gain_one, "dp", scatter_dimension=0, tiled=True),
-        lax.psum_scatter(grad_weight_qkv, "dp", scatter_dimension=0, tiled=True),
-        lax.psum_scatter(grad_weight_attn, "dp", scatter_dimension=1, tiled=True),
-        lax.psum_scatter(grad_gain_two, "dp", scatter_dimension=0, tiled=True),
-        lax.psum_scatter(grad_weight_in, "dp", scatter_dimension=0, tiled=True),
-        lax.psum_scatter(grad_weight_out, "dp", scatter_dimension=1, tiled=True),
-    )
-    owned_qkv, owned_attn, owned_in, owned_out = (
-        lax.psum_scatter(
-            owned_qkv.astype(jnp.bfloat16), "tensor", scatter_dimension=2, tiled=True
-        ).astype(jnp.float32),
-        lax.psum_scatter(
-            owned_attn.astype(jnp.bfloat16), "tensor", scatter_dimension=0, tiled=True
-        ).astype(jnp.float32),
-        lax.psum_scatter(
-            owned_in.astype(jnp.bfloat16), "tensor", scatter_dimension=2, tiled=True
-        ).astype(jnp.float32),
-        lax.psum_scatter(
-            owned_out.astype(jnp.bfloat16), "tensor", scatter_dimension=0, tiled=True
-        ).astype(jnp.float32),
-    )
+    grad_in = grad_weight_in.reshape(width, 2, 2, half_units).transpose(2, 0, 1, 3)
+    grad_in = own_half(grad_in.reshape(2, width, 2 * half_units))
+    grad_down = jnp.concatenate(
+        [
+            grad_weight_attn.reshape(2, half_width, width),
+            grad_weight_out.reshape(2, half_units, width),
+        ],
+        axis=1,
+    ).transpose(0, 2, 1)
+    grad_down = own_half(grad_down)
+    grad_parts = grad_weight_qkv.reshape(width, 3, 2, half_width).transpose(2, 0, 1, 3)
+    grad_query_key = own_half(grad_parts[:, :, :2].reshape(2, width, 2 * half_width))
+    grad_gains = jnp.pad(jnp.stack([grad_gain_one, grad_gain_two], axis=1), ((0, 0), (0, 126)))
+    grad_value = own_half(
+        jnp.concatenate([grad_parts[:, :, 2], jnp.stack([grad_gains, grad_gains])], axis=2)
+    )
+    owned_in = scatter_rows(grad_in, False).reshape(own_rows, 2, half_units)
+    owned_down = scatter_rows(grad_down, True)
+    owned_attn = owned_down[:, :half_width].T
+    owned_out = owned_down[:, half_width:].T
+    owned_query_key = scatter_rows(grad_query_key, False)
+    owned_value = scatter_rows(grad_value, True)
+    owned_qkv = jnp.concatenate(
+        [
+            owned_query_key.reshape(own_rows, 2, half_width),
+            owned_value[:, None, :half_width],
+        ],
+        axis=1,
+    )
+    owned_gain_one = owned_value[:, half_width]
+    owned_gain_two = owned_value[:, half_width + 1]
     return (
         layer_out,
         grad_tokens,

time: 1020 us -> 762 us (0.75)
  waiting for transfers between devices: 332 us -> 71.2 us
  blocking collectives: 175 us -> 0 us
  local copies, waits for them, and re-layouts: 151 us -> 247 us
  other arithmetic: 199 us -> 255 us
  starting transfers between devices: 10.5 us -> 50.3 us
  between operations: 16.5 us -> 2.61 us
    reduce_scatter x4 -> x0, waiting for transfers between devices: 316 us -> none  [the longest x1 153 us: body(): lax.psum_scatter(grad_weight_in, 'dp', scatter_dimension=0, tiled=True)]
    all_gather x2 -> x0, blocking collectives: 94.7 us -> none  [the longest x1 49.8 us: body(): lax.all_gather(out_weight, 'dp', axis=1, tiled=True)]
    unnamed x2 -> x0, blocking collectives: 76.9 us -> none
    ppermute x0 -> x40, waiting for transfers between devices: none -> 71.2 us  [the longest x32 71.2 us: exchanged(): return lax.ppermute(block, 'dp', [(i, i ^ mask) for i in range(devices)])]
    ppermute x0 -> x40, starting transfers between devices: none -> 41.2 us  [the longest x32 37.4 us: exchanged(): return lax.ppermute(block, 'dp', [(i, i ^ mask) for i in range(devices)])]
    transpose x0 -> x9, local copies, waits for them, and re-layouts: none -> 35.2 us  [the longest x1 11.1 us: body(): up.reshape(2, width, 2, half_units).transpose(1, 2, 0, 3)]
    select_n x0 -> x19, other arithmetic: none -> 26.2 us  [the longest x3 16.8 us: both_halves(): return jnp.where(first, jnp.stack([own, other]), jnp.stack([other, own]))]
    add x0 -> x18, other arithmetic: none -> 21.5 us  [the longest x4 11.3 us: own_half(): keep.astype(jnp.float32)]
  transfers between devices with their start and end apart: 18 -> 44, of which waited for: 4 -> 16; matrix products, arithmetic and copies ran while one was open for 41% -> 39% of each run, Pallas kernels for 0% -> 0%
where the time goes in v1:
time: 762 us; the launch traced here: 750 us
  other arithmetic  255 us (33%)
  local copies, waits for them, and re-layouts  247 us (32%)
  matrix products  124 us (16%)
  waiting for transfers between devices  71.2 us (9%)
  starting transfers between devices  50.3 us (7%)
    sub x1, other arithmetic, one_block(): grad_scores = (probs * (grad_probs - delta)).astype(jnp.bfloat16)  92.1 us
    ppermute x32, waiting for transfers between devices, exchanged(): return lax.ppermute(block, 'dp', [(i, i ^ mask) for i in range(devices)])  71.2 us
    unnamed x199, local copies, waits for them, and re-layouts  49.1 us
    ppermute x32, starting transfers between devices, exchanged(): return lax.ppermute(block, 'dp', [(i, i ^ mask) for i in range(devices)])  37.4 us
    dot_general x1, matrix products, body(): jnp.dot(gated_low, weight_out, preferred_element_type=jnp.float32)  18 us
    select_n x3, other arithmetic, both_halves(): return jnp.where(first, jnp.stack([own, other]), jnp.stack([other, own]))  16.8 us
  transfers between devices with their start and end apart: 44, of which 16 were waited for; matrix products, arithmetic and copies ran while one was open for 39% of the time, Pallas kernels for 0%

profile of v1, /device:TPU:0, one launch (start us, length us, event | category | flops | bytes accessed | tf_op | source)
XLA Modules:
  0.0 750.1 jit_solution(9869218511204803461)
XLA Ops:
  40.1 13.2 %collective-permute-done.1 = bf16[1,2,1,1,48,512]{5,4,3,2,1,0:T(8,128)(2,1)S(1)} collective-permute-done((bf16[1,2,1,1,48,512]{5,4,3,2,1,0:T(8,128)(2,1)S(1)}, bf16[1,2,1,1,48,512]{5,4,3,2,1,0:T(8,128)(2,1)S(1)}, u32[]{:S(2)}, u32[]{:S(2)}) %collective-permute-start.1) | collective-permute-done | bytes 98336 | tf_op jit(solution)/shard_map/ppermute | solution.py:156
  91.8 8.1 %broadcast_select_fusion.1 = bf16[2,768,1,384]{3,2,1,0:T(2,128)(2,1)} fusion(pred[]{:T(512)S(6)} %eq.74, bf16[1,768,1,384]{3,2,1,0:T(2,128)(2,1)S(1)} %copy.311, bf16[1,768,1,384]{3,2,1,0:T(2,128)(2,1)S(1)} %copy.310), kind=kLoop, calls=%fused_computation.98 | loop fusion | flops 1769472 | bytes 2359297 | tf_op jit(solution)/shard_map/jit(_where)/select_n | solution.py:198
  129.6 8.0 %copy.314 = bf16[768,3,2,384]{0,3,2,1:T(8,128)(2,1)} copy(bf16[768,3,2,384]{3,1,0,2:T(4,128)(2,1)} %maximum_bitcast_fusion) | data formatting | bytes 7077888 | tf_op jit(solution)/shard_map/transpose | solution.py:238
  137.6 7.2 fusion.111
  173.3 7.4 fusion.16
  180.7 8.2 %pad_maximum_fusion.6 = (bf16[1152,1,12,64]{0,3,2,1:T(8,128)(2,1)}, bf16[1152,1,12,64]{0,3,2,1:T(8,128)(2,1)}, bf16[1152,1,12,64]{0,3,2,1:T(8,128)(2,1)}, bf16[1152,1,12,64]{0,3,2,1:T(8,128)(2,1)}) fusion(bf16[64,2,12,64]{0,3,2,1:T(8,128)(2,1)} %collective-permute-done.11, bf16[1152,1,12,64]{0,3,2,1:T(8,128)(2,1)S(1)} %bitcast.374, ...), kind=kLoop, calls=%fused_computation.172 | loop fusion | flops 21233664 | bytes 11010048 | tf_op jit(solution)/shard_map/concatenate | solution.py:266
  202.2 7.2 fusion.189
  214.3 8.0 %fusion.5 = (bf16[12,9,128,256]{3,2,1,0:T(8,128)(2,1)}, bf16[12,9,128,256]{3,2,1,0:T(8,128)(2,1)}) fusion(f32[12,9,128,256]{3,2,1,0:T(8,128)S(1)} %get-tuple-element.178, f32[12,9,128]{2,1,0:T(8,128)S(1)} %log_add_fusion, f32[12,9,128]{2,1,0:T(8,128)S(1)} %fusion.4, f32[12,9,128]{2,1,0:T(8,128)S(1)} %get-tuple-element.177), kind=kLoop, calls=%fused_computation.9 | loop fusion | flops 17694720 | bytes 28477440 | tf_op jit(solution)/shard_map/while/body/eval_jaxpr/convert_element_type | solution.py:109
  276.4 11.1 %fusion.58 = bf16[768,2,2,576]{3,1,0,2:T(2,128)(2,1)} fusion(pred[]{:T(512)S(6)} %eq.74, bf16[1,768,2,576]{3,2,1,0:T(2,128)(2,1)} %copy.330, bf16[1,768,2,576]{3,2,1,0:T(2,128)(2,1)S(1)} %copy-done.39), kind=kLoop, calls=%fused_computation.104 | loop fusion | flops 5308416 | bytes 7077889 | tf_op jit(solution)/shard_map/transpose | solution.py:239
  287.4 11.1 %copy.332 = bf16[768,2,2,576]{0,3,2,1:T(8,128)(2,1)} copy(bf16[768,2,2,576]{3,1,0,2:T(2,128)(2,1)} %fusion.58) | data formatting | bytes 7077888 | tf_op jit(solution)/shard_map/transpose | solution.py:239
  298.5 7.4 fusion.180
  306.0 12.3 %fusion.26 = (bf16[1152,1152]{0,1:T(8,128)(2,1)}, f32[1152,1152]{0,1:T(8,128)S(1)}) fusion(f32[1152,2,1152]{0,2,1:T(8,128)S(1)} %fusion.180), kind=kLoop, calls=%fused_computation.46 | loop fusion | flops 87588864 | bytes 18579456 | tf_op jit(solution)/shard_map/convert_element_type | solution.py:281
  318.3 18.0 %fusion.69 = bf16[1152,768]{0,1:T(8,128)(2,1)} fusion(f32[1152,768]{0,1:T(8,128)S(1)} %copy-done.23, bf16[1152,768]{1,0:T(8,128)(2,1)S(1)} %bitcast.405, f32[1152,2,1152]{0,2,1:T(8,128)S(1)} %fusion.180), kind=kOutput, calls=%fused_computation.146 | convolution fusion | flops 2127790080 | bytes 17694720 | tf_op jit(solution)/shard_map/dot_general | solution.py:283
  336.3 8.7 %multiply_bitcast_fusion.1 = (f32[1152,1,1152]{0,2,1:T(8,128)}, f32[1152,1,1152]{0,2,1:T(8,128)}) fusion(f32[1152,1152]{0,1:T(8,128)S(1)} %get-tuple-element.114, f32[1152,2,1152]{0,2,1:T(8,128)S(1)} %fusion.180, bf16[1152,768]{1,0:T(8,128)(2,1)} %bitcast.404, bf16[1152,768]{0,1:T(8,128)(2,1)S(1)} %copy-done.15, f32[1152]{0:T(1024)S(1)} %copy-done.70), kind=kOutput, calls=%fused_computation.62 | convolution fusion | flops 2062319616 | bytes 30085632 | tf_op jit(solution)/shard_map/rd,fd->rf/dot_general | solution.py:290
  345.1 11.7 %multiply_reduce_fusion.1 = (f32[768]{0:T(1024)}, f32[1152]{0:T(1024)S(1)}, f32[1152,768]{0,1:T(8,128)S(1)}) fusion(f32[1152,768]{0,1:T(8,128)S(1)} %copy-done.23, f32[1152]{0:T(1024)S(1)} %copy-done.84, f32[1152]{0:T(1024)S(1)} %broadcast_multiply_fusion.2, f32[768]{0:T(1024)S(1)} %copy-done.85, bf16[768,2,1152]{0,2,1:T(8,128)(2,1)} %bitcast.400, ...), kind=kOutput, calls=%fused_computation.136 | convolution fusion | flops 4088363008 | bytes 21253632 | tf_op jit(solution)/shard_map/rcf,dcf->rd/dot_general | solution.py:297
  379.7 9.0 %fusion.66 = f32[12,9,128,256]{3,2,1,0:T(8,128)} fusion(bf16[9,256,12,64]{1,3,2,0:T(8,128)(2,1)S(1)} %copy-done.10, bf16[9,128,12,64]{1,0,3,2:T(8,128)(2,1)} %reshape_reshape.19), kind=kOutput, calls=%fused_computation.133 | convolution fusion | flops 452984832 | bytes 19464192 | tf_op jit(solution)/shard_map/while/body/eval_jaxpr/sqhd,skhd->hsqk/dot_general | solution.py:111
  388.7 92.1 %multiply_convert_fusion = bf16[12,9,128,256]{3,2,1,0:T(8,128)(2,1)} fusion(f32[12,9,128,256]{3,2,1,0:T(8,128)} %fusion.66, f32[12,9,128,256]{3,2,1,0:T(8,128)} %copy-done, f32[12,9,128]{2,1,0:T(8,128)S(1)} %copy-done.62), kind=kOutput, calls=%fused_computation.1 | output fusion | flops 21247744 | bytes 35444736 | tf_op jit(solution)/shard_map/while/body/eval_jaxpr/sub | solution.py:115
  480.8 9.6 %multiply_bitcast_fusion.3 = (f32[9,128,12,64]{1,3,2,0:T(8,128)}, f32[9,12,8,8,128]{4,3,2,1,0:T(8,128)}) fusion(bf16[12,9,128,256]{3,2,1,0:T(8,128)(2,1)} %multiply_convert_fusion, bf16[9,256,12,64]{1,3,0,2:T(8,128)(2,1)} %copy_dynamic-update-slice_fusion), kind=kOutput, calls=%fused_computation.151 | convolution fusion | flops 453869568 | bytes 17694720 | tf_op jit(solution)/shard_map/while/body/eval_jaxpr/hsqk,skhd->sqhd/dot_general | solution.py:118
  536.4 7.7 %reshape.2556 = f32[1152,1,768]{2,0,1:T(8,128)} reshape(f32[9,128,12,64]{3,2,1,0:T(8,128)} %copy.396) | data formatting | bytes 7077888 | tf_op jit(solution)/shard_map/reshape | solution.py:137
  578.4 7.5 %add_convert_fusion.2 = (bf16[1152,1,768]{2,0,1:T(8,128)(2,1)S(1)}, bf16[1152,1,768]{2,0,1:T(8,128)(2,1)S(1)}) fusion(f32[1152,1,768]{2,0,1:T(8,128)} %copy.350, f32[1152,1,768]{2,0,1:T(8,128)} %reshape.2556, f32[1152,1,768]{2,0,1:T(8,128)} %copy.348, f32[1152,1,768]{2,0,1:T(8,128)} %copy.361, f32[1152,1,768]{2,0,1:T(8,128)} %copy.359), kind=kLoop, calls=%fused_computation.139 | loop fusion | flops 5308416 | bytes 21233664 | tf_op jit(solution)/shard_map/convert.6
  592.1 7.3 fusion.82
  600.9 8.4 %copy.366 = f32[768,3,2,384]{3,0,2,1:T(8,128)} copy(f32[768,3,2,384]{0,3,2,1:T(8,128)} %bitcast.391) | data formatting | bytes 14155776 | tf_op jit(solution)/shard_map/reshape | solution.py:347
  690.4 10.2 %collective-permute-done.31 = bf16[2,2,1,1,48,768]{5,4,3,2,1,0:T(8,128)(2,1)} collective-permute-done((bf16[2,2,1,1,48,768]{5,4,3,2,1,0:T(8,128)(2,1)}, bf16[2,2,1,1,48,768]{5,4,3,2,1,0:T(8,128)(2,1)}, u32[]{:S(2)}, u32[]{:S(2)}) %collective-permute-start.31) | collective-permute-done | bytes 294944 | tf_op jit(solution)/shard_map/ppermute | solution.py:156
  734.6 9.2 %collective-permute-done.42 = bf16[1,2,1,1,48,1152]{5,4,3,2,1,0:T(8,128)(2,1)S(1)} collective-permute-done((bf16[1,2,1,1,48,1152]{5,4,3,2,1,0:T(8,128)(2,1)S(1)}, bf16[1,2,1,1,48,1152]{5,4,3,2,1,0:T(8,128)(2,1)S(1)}, u32[]{:S(2)}, u32[]{:S(2)}) %collective-permute-start.42) | collective-permute-done | bytes 221216 | tf_op jit(solution)/shard_map/ppermute | solution.py:156
  (475 shorter events, 438.9 us)
Async XLA Ops:
  2.2 31.4 %collective-permute-start = (bf16[1,1,1,1,48,512]{5,4,3,2,1,0:T(8,128)(2,1)S(1)}, bf16[1,1,1,1,48,512]{5,4,3,2,1,0:T(8,128)(2,1)S(1)}, u32[]{:S(2)}, u32[]{:S(2)}) collective-permute-start(bf16[1,1,1,1,48,512]{5,4,3,2,1,0:T(8,128)(2,1)S(1)} %get-tuple-element.172), channel_id=1, source_target_pairs={{0,8},{2,10},{4,12},{6,14},{8,0},{10,2},{12,4},{14,6},{16,24},{18,... | collective-permute-start | bytes 147464 | tf_op jit(solution)/shard_map/ppermute | solution.py:156
  6.3 30.4 %collective-permute-start.4 = (bf16[1,1,1,1,48,768]{5,4,3,2,1,0:T(8,128)(2,1)S(1)}, bf16[1,1,1,1,48,768]{5,4,3,2,1,0:T(8,128)(2,1)S(1)}, u32[]{:S(2)}, u32[]{:S(2)}) collective-permute-start(bf16[1,1,1,1,48,768]{5,4,3,2,1,0:T(8,128)(2,1)S(1)} %reshape_reshape.17), channel_id=1, source_target_pairs={{0,8},{2,10},{4,12},{6,14},{8,0},{10,2},{12,4},{14,6},{16,24},{18,... | collective-permute-start | bytes 221192 | tf_op jit(solution)/shard_map/ppermute | solution.py:156
  7.4 32.5 %collective-permute-start.17 = (bf16[1,1,1,1,48,1152]{5,4,3,2,1,0:T(8,128)(2,1)S(1)}, bf16[1,1,1,1,48,1152]{5,4,3,2,1,0:T(8,128)(2,1)S(1)}, u32[]{:S(2)}, u32[]{:S(2)}) collective-permute-start(bf16[1,1,1,1,48,1152]{5,4,3,2,1,0:T(8,128)(2,1)S(1)} %reshape_reshape.18), channel_id=1, source_target_pairs={{0,8},{2,10},{4,12},{6,14},{8,0},{10,2},{12,4},{14,6},{16,24},{18,... | collective-permute-start | bytes 331784 | tf_op jit(solution)/shard_map/ppermute | solution.py:156
  10.4 26.5 %collective-permute-start.12 = (bf16[1,1,1,1,48,960]{5,4,3,2,1,0:T(8,128)(2,1)S(1)}, bf16[1,1,1,1,48,960]{5,4,3,2,1,0:T(8,128)(2,1)S(1)}, u32[]{:S(2)}, u32[]{:S(2)}) collective-permute-start(bf16[1,1,1,1,48,960]{5,4,3,2,1,0:T(8,128)(2,1)S(1)} %get-tuple-element.167), channel_id=1, source_target_pairs={{0,8},{2,10},{4,12},{6,14},{8,0},{10,2},{12,4},{14,6},{16,24},{18,... | collective-permute-start | bytes 276488 | tf_op jit(solution)/shard_map/ppermute | solution.py:156
  33.6 19.7 %collective-permute-start.1 = (bf16[1,2,1,1,48,512]{5,4,3,2,1,0:T(8,128)(2,1)S(1)}, bf16[1,2,1,1,48,512]{5,4,3,2,1,0:T(8,128)(2,1)S(1)}, u32[]{:S(2)}, u32[]{:S(2)}) collective-permute-start(bf16[1,2,1,1,48,512]{5,4,3,2,1,0:T(8,128)(2,1)S(1)} %maximum_select_fusion.22), channel_id=1, source_target_pairs={{0,16},{2,18},{4,20},{6,22},{8,24},{10,26},{12,28},{14,30},{16,0},... | collective-permute-start | bytes 294920 | tf_op jit(solution)/shard_map/ppermute | solution.py:156
  36.7 19.7 %collective-permute-start.5 = (bf16[1,2,1,1,48,768]{5,4,3,2,1,0:T(8,128)(2,1)S(1)}, bf16[1,2,1,1,48,768]{5,4,3,2,1,0:T(8,128)(2,1)S(1)}, u32[]{:S(2)}, u32[]{:S(2)}) collective-permute-start(bf16[1,2,1,1,48,768]{5,4,3,2,1,0:T(8,128)(2,1)S(1)} %maximum_select_fusion.20), channel_id=1, source_target_pairs={{0,16},{2,18},{4,20},{6,22},{8,24},{10,26},{12,28},{14,30},{16,0},... | collective-permute-start | bytes 442376 | tf_op jit(solution)/shard_map/ppermute | solution.py:156
  36.9 23.8 %collective-permute-start.13 = (bf16[1,2,1,1,48,960]{5,4,3,2,1,0:T(8,128)(2,1)S(1)}, bf16[1,2,1,1,48,960]{5,4,3,2,1,0:T(8,128)(2,1)S(1)}, u32[]{:S(2)}, u32[]{:S(2)}) collective-permute-start(bf16[1,2,1,1,48,960]{5,4,3,2,1,0:T(8,128)(2,1)S(1)} %maximum_select_fusion.18), channel_id=1, source_target_pairs={{0,16},{2,18},{4,20},{6,22},{8,24},{10,26},{12,28},{14,30},{16,0},... | collective-permute-start | bytes 552968 | tf_op jit(solution)/shard_map/ppermute | solution.py:156
  39.9 24.7 %collective-permute-start.18 = (bf16[1,2,1,1,48,1152]{5,4,3,2,1,0:T(8,128)(2,1)S(1)}, bf16[1,2,1,1,48,1152]{5,4,3,2,1,0:T(8,128)(2,1)S(1)}, u32[]{:S(2)}, u32[]{:S(2)}) collective-permute-start(bf16[1,2,1,1,48,1152]{5,4,3,2,1,0:T(8,128)(2,1)S(1)} %maximum_select_fusion.15), channel_id=1, source_target_pairs={{0,16},{2,18},{4,20},{6,22},{8,24},{10,26},{12,28},{14,30},{16,0},... | collective-permute-start | bytes 663560 | tf_op jit(solution)/shard_map/ppermute | solution.py:156
  66.7 19.5 %collective-permute-start.7 = (bf16[2,2,2,1,48,768]{5,4,3,2,1,0:T(8,128)(2,1)S(1)}, bf16[2,2,2,1,48,768]{5,4,3,2,1,0:T(8,128)(2,1)S(1)}, u32[]{:S(2)}, u32[]{:S(2)}) collective-permute-start(bf16[2,2,2,1,48,768]{5,4,3,2,1,0:T(8,128)(2,1)S(1)} %maximum_select_fusion.7), channel_id=1, source_target_pairs={{0,2},{2,0},{4,6},{6,4},{8,10},{10,8},{12,14},{14,12},{16,18},{18,... | collective-permute-start | bytes 1769480 | tf_op jit(solution)/shard_map/ppermute | solution.py:156
  76.9 23.1 %collective-permute-start.15 = (bf16[2,2,1,2,48,960]{5,4,3,2,1,0:T(8,128)(2,1)}, bf16[2,2,1,2,48,960]{5,4,3,2,1,0:T(8,128)(2,1)}, u32[]{:S(2)}, u32[]{:S(2)}) collective-permute-start(bf16[2,2,1,2,48,960]{5,4,3,2,1,0:T(8,128)(2,1)} %maximum_select_fusion.6), channel_id=1, source_target_pairs={{0,4},{2,6},{4,0},{6,2},{8,12},{10,14},{12,8},{14,10},{16,20},{18,... | collective-permute-start | bytes 2211848 | tf_op jit(solution)/shard_map/ppermute | solution.py:156
  84.7 20.0 %collective-permute-start.20 = (bf16[2,2,2,1,48,1152]{5,4,3,2,1,0:T(8,128)(2,1)}, bf16[2,2,2,1,48,1152]{5,4,3,2,1,0:T(8,128)(2,1)}, u32[]{:S(2)}, u32[]{:S(2)}) collective-permute-start(bf16[2,2,2,1,48,1152]{5,4,3,2,1,0:T(8,128)(2,1)} %maximum_select_fusion.4), channel_id=1, source_target_pairs={{0,2},{2,0},{4,6},{6,4},{8,10},{10,8},{12,14},{14,12},{16,18},{18,... | collective-permute-start | bytes 2654216 | tf_op jit(solution)/shard_map/ppermute | solution.py:156
  90.9 22.8 %collective-permute-start.8 = (bf16[768,768]{1,0:T(8,128)(2,1)}, bf16[768,768]{1,0:T(8,128)(2,1)}, u32[]{:S(2)}, u32[]{:S(2)}) collective-permute-start(bf16[768,768]{1,0:T(8,128)(2,1)} %bitcast.24), channel_id=1, source_target_pairs={{0,1},{1,0},{2,3},{3,2},{4,5},{5,4},{6,7},{7,6},{8,9},{9,8},{10,11... | collective-permute-start | bytes 3538952 | tf_op jit(solution)/shard_map/ppermute | solution.py:160
  104.1 140.0 %collective-permute-start.16 = (bf16[768,960]{0,1:T(8,128)(2,1)}, bf16[768,960]{0,1:T(8,128)(2,1)}, u32[]{:S(2)}, u32[]{:S(2)}) collective-permute-start(bf16[768,960]{0,1:T(8,128)(2,1)} %copy.326), channel_id=1, source_target_pairs={{0,1},{1,0},{2,3},{3,2},{4,5},{5,4},{6,7},{7,6},{8,9},{9,8},{10,11... | collective-permute-start | bytes 4423688 | tf_op jit(solution)/shard_map/ppermute | solution.py:160
  113.7 152.1 %collective-permute-start.21 = (bf16[768,1152]{1,0:T(8,128)(2,1)}, bf16[768,1152]{1,0:T(8,128)(2,1)}, u32[]{:S(2)}, u32[]{:S(2)}) collective-permute-start(bf16[768,1152]{1,0:T(8,128)(2,1)} %bitcast.392), channel_id=1, source_target_pairs={{0,1},{1,0},{2,3},{3,2},{4,5},{5,4},{6,7},{7,6},{8,9},{9,8},{10,11... | collective-permute-start | bytes 5308424 | tf_op jit(solution)/shard_map/ppermute | solution.py:160
  151.3 29.4 %collective-permute-start.11 = (bf16[64,2,12,64]{0,3,2,1:T(8,128)(2,1)}, bf16[64,2,12,64]{0,3,2,1:T(8,128)(2,1)}, u32[]{:S(2)}, u32[]{:S(2)}) collective-permute-start(bf16[64,2,12,64]{0,3,2,1:T(8,128)(2,1)} %get-tuple-element.147), channel_id=1, source_target_pairs={{1,0},{3,2},{5,4},{7,6},{9,8},{11,10},{13,12},{15,14},{17,16},{19,... | collective-permute-start | bytes 589832 | tf_op jit(solution)/shard_map/ppermute | solution.py:15
  152.6 28.2 %collective-permute-start.10 = (bf16[64,2,12,64]{0,3,2,1:T(8,128)(2,1)}, bf16[64,2,12,64]{0,3,2,1:T(8,128)(2,1)}, u32[]{:S(2)}, u32[]{:S(2)}) collective-permute-start(bf16[64,2,12,64]{0,3,2,1:T(8,128)(2,1)} %get-tuple-element.148), channel_id=1, source_target_pairs={{0,1},{2,3},{4,5},{6,7},{8,9},{10,11},{12,13},{14,15},{16,17},{18,... | collective-permute-start | bytes 589832 | tf_op jit(solution)/shard_map/ppermute | solution.py:15
  514.3 29.7 %collective-permute-start.22 = (bf16[64,2,12,64]{0,3,2,1:T(8,128)(2,1)}, bf16[64,2,12,64]{0,3,2,1:T(8,128)(2,1)}, u32[]{:S(2)}, u32[]{:S(2)}) collective-permute-start(bf16[64,2,12,64]{0,3,2,1:T(8,128)(2,1)} %get-tuple-element.129), channel_id=1, source_target_pairs={{0,1},{2,3},{4,5},{6,7},{8,9},{10,11},{12,13},{14,15},{16,17},{18,... | collective-permute-start | bytes 589832 | tf_op jit(solution)/shard_map/ppermute | solution.py:15
  516.4 27.7 %collective-permute-start.23 = (bf16[64,2,12,64]{0,3,2,1:T(8,128)(2,1)}, bf16[64,2,12,64]{0,3,2,1:T(8,128)(2,1)}, u32[]{:S(2)}, u32[]{:S(2)}) collective-permute-start(bf16[64,2,12,64]{0,3,2,1:T(8,128)(2,1)} %get-tuple-element.130), channel_id=1, source_target_pairs={{1,0},{3,2},{5,4},{7,6},{9,8},{11,10},{13,12},{15,14},{17,16},{19,... | collective-permute-start | bytes 589832 | tf_op jit(solution)/shard_map/ppermute | solution.py:15
  613.1 19.6 %collective-permute-start.24 = (bf16[768,512]{1,0:T(8,128)(2,1)S(1)}, bf16[768,512]{1,0:T(8,128)(2,1)}, u32[]{:S(2)}, u32[]{:S(2)}) collective-permute-start(bf16[768,512]{1,0:T(8,128)(2,1)S(1)} %fusion.108), channel_id=1, source_target_pairs={{0,1},{1,0},{2,3},{3,2},{4,5},{5,4},{6,7},{7,6},{8,9},{9,8},{10,11... | collective-permute-start | bytes 2359304 | tf_op jit(solution)/shard_map/ppermute | solution.py:160
  616.3 47.0 %collective-permute-start.34 = (bf16[768,960]{0,1:T(8,128)(2,1)}, bf16[768,960]{0,1:T(8,128)(2,1)}, u32[]{:S(2)}, u32[]{:S(2)}) collective-permute-start(bf16[768,960]{0,1:T(8,128)(2,1)} %fusion.106), channel_id=1, source_target_pairs={{0,1},{1,0},{2,3},{3,2},{4,5},{5,4},{6,7},{7,6},{8,9},{9,8},{10,11... | collective-permute-start | bytes 4423688 | tf_op jit(solution)/shard_map/ppermute | solution.py:160
  620.5 60.3 %collective-permute-start.39 = (bf16[768,1152]{0,1:T(8,128)(2,1)}, bf16[768,1152]{0,1:T(8,128)(2,1)}, u32[]{:S(2)}, u32[]{:S(2)}) collective-permute-start(bf16[768,1152]{0,1:T(8,128)(2,1)} %fusion.85), channel_id=1, source_target_pairs={{0,1},{1,0},{2,3},{3,2},{4,5},{5,4},{6,7},{7,6},{8,9},{9,8},{10,11... | collective-permute-start | bytes 5308424 | tf_op jit(solution)/shard_map/ppermute | solution.py:160
  675.5 26.7 %collective-permute-start.35 = (bf16[2,2,1,2,48,960]{5,4,3,2,1,0:T(8,128)(2,1)}, bf16[2,2,1,2,48,960]{5,4,3,2,1,0:T(8,128)(2,1)}, u32[]{:S(2)}, u32[]{:S(2)}) collective-permute-start(bf16[2,2,1,2,48,960]{5,4,3,2,1,0:T(8,128)(2,1)} %dynamic-slice_convert_fusion.3), channel_id=1, source_target_pairs={{0,4},{2,6},{4,0},{6,2},{8,12},{10,14},{12,8},{14,10},{16,20},{18,... | collective-permute-start | bytes 2211848 | tf_op jit(solution)/shard_map/ppermute | solution.py:156
  679.7 20.9 %collective-permute-start.31 = (bf16[2,2,1,1,48,768]{5,4,3,2,1,0:T(8,128)(2,1)}, bf16[2,2,1,1,48,768]{5,4,3,2,1,0:T(8,128)(2,1)}, u32[]{:S(2)}, u32[]{:S(2)}) collective-permute-start(bf16[2,2,1,1,48,768]{5,4,3,2,1,0:T(8,128)(2,1)} %dynamic-slice_convert_fusion.8), channel_id=1, source_target_pairs={{0,4},{2,6},{4,0},{6,2},{8,12},{10,14},{12,8},{14,10},{16,20},{18,... | collective-permute-start | bytes 884744 | tf_op jit(solution)/shard_map/ppermute | solution.py:156
  689.3 30.6 %collective-permute-start.40 = (bf16[2,2,2,1,48,1152]{5,4,3,2,1,0:T(8,128)(2,1)}, bf16[2,2,2,1,48,1152]{5,4,3,2,1,0:T(8,128)(2,1)}, u32[]{:S(2)}, u32[]{:S(2)}) collective-permute-start(bf16[2,2,2,1,48,1152]{5,4,3,2,1,0:T(8,128)(2,1)} %dynamic-slice_convert_fusion.2), channel_id=1, source_target_pairs={{0,2},{2,0},{4,6},{6,4},{8,10},{10,8},{12,14},{14,12},{16,18},{18,... | collective-permute-start | bytes 2654216 | tf_op jit(solution)/shard_map/ppermute | solution.py:156
  (115 other events, 1313.7 us)

commit v2 on v0

v2 whole, which is shorter than its diff:
```python
import jax
import jax.numpy as jnp
from jax import lax
from jax.experimental import pallas as pl
from jax.experimental.pallas import tpu as pltpu
from jax.sharding import PartitionSpec as P

HEAD_DIM = 64
WINDOW_HALF = 64
PAD_BLOCK = 128
WIDTH = 768
ROWS = 1152
HALF = 1152
LANES = 128
PAIRS = 6
SPAN = 2 * LANES
UNITS = 512
FIRST_CUT = 640
DOWN = 384 + UNITS + LANES
VMEM = 58 * 2**20
F32 = jnp.float32
BF16 = jnp.bfloat16


def steps_of(devices, swapped):
    bits = [1 << i for i in range(devices.bit_length() - 1)]
    near, far = bits[:2], bits[2:]
    return far + (near if swapped else near[::-1])


def exchanged(block, mask):
    devices = lax.axis_size("dp")
    return lax.ppermute(block, "dp", [(i, i ^ mask) for i in range(devices)])


def swapped_cores(block):
    return lax.ppermute(block, "tensor", [(0, 1), (1, 0)])


def by_exchange(own_rows):
    devices = lax.axis_size("dp")
    return own_rows % 16 == 0 and devices & (devices - 1) == 0


def relative(own_rows, swapped):
    if not by_exchange(own_rows):
        return list(range(WIDTH // 48))
    order = [0]
    for mask in steps_of(lax.axis_size("dp"), swapped):
        order = order + [r ^ mask for r in order]
    return order


def gather_slots(shard, swapped):
    if not by_exchange(shard.shape[0]):
        whole = lax.all_gather(shard, "dp", axis=0, tiled=True)
        return [whole.reshape(WIDTH // 48, 48, shard.shape[1])]
    held = shard[None]
    masks = steps_of(lax.axis_size("dp"), swapped)
    for mask in masks[:-1]:
        held = jnp.concatenate([held, exchanged(held, mask)], axis=0)
    return [held, exchanged(held, masks[-1])]


def scatter_slots(keep, send, own_rows, swapped):
    other = swapped_cores(send)
    if not by_exchange(own_rows):
        total = keep.astype(F32) + other.astype(F32)
        total = total.reshape(WIDTH, keep.shape[2])
        return lax.psum_scatter(total, "dp", scatter_dimension=0, tiled=True)
    for mask in reversed(steps_of(lax.axis_size("dp"), swapped)):
        middle = keep.shape[0] // 2
        kept = keep[:middle].astype(F32) + other[:middle].astype(F32)
        sent = keep[middle:].astype(F32) + other[middle:].astype(F32)
        other = exchanged(sent.astype(BF16), mask)
        keep = kept
    return (keep + other.astype(F32))[0]


def scatter_gains(first, second):
    devices = lax.axis_size("dp")
    index = lax.axis_index("dp")
    levels = devices.bit_length() - 1
    part = WIDTH // devices
    both = jnp.stack([first, second]).reshape(2, devices, part).transpose(1, 0, 2)
    if devices & (devices - 1):
        both = lax.psum(both, "tensor")
        held = lax.psum_scatter(both, "dp", scatter_dimension=0, tiled=True)[0]
        return held[0], held[1]
    held = jnp.pad(both, ((0, 0), (0, 6), (0, LANES - part)))
    held = held + swapped_cores(held)
    held = held.reshape((2,) * levels + (8, LANES))
    for mask in reversed(steps_of(devices, False)):
        axis = levels - mask.bit_length()
        bit = (index & mask) // mask
        keep = lax.dynamic_slice_in_dim(held, bit, 1, axis)
        held = keep + exchanged(lax.dynamic_slice_in_dim(held, 1 - bit, 1, axis), mask)
    held = held.reshape(8, LANES)
    return held[0, :part], held[1, :part]


def nt(left, right):
    return lax.dot_general(left, right, (((1,), (1,)), ((), ())), preferred_element_type=F32)


def tn(left, right):
    return lax.dot_general(left, right, (((0,), (0,)), ((), ())), preferred_element_type=F32)


def nn(left, right):
    return jnp.dot(left, right, preferred_element_type=F32)


def start_slots(info, pieces, order, segments, sems):
    half = len(pieces) // 2
    slot = 0
    for number, piece in enumerate(pieces):
        if number == half:
            slot = 0
        mine = number < half
        core = info[1] if mine else 1 - info[1]
        rows = piece.shape[1]
        for at in range(piece.shape[0]):
            row = pl.multiple_of((info[0] ^ order[slot]) * rows, 16)
            for begin, width, own, other in segments:
                target = own if mine else other
                if target is None:
                    continue
                ref, sem, stride, offset = target
                column = pl.multiple_of(core * stride + offset, LANES)
                pltpu.make_async_copy(
                    piece.at[at, :, pl.ds(begin, width)],
                    ref.at[pl.ds(row, rows), pl.ds(column, width)],
                    sems.at[sem],
                ).start()
            slot += 1


def wait_whole(ref, sem):
    pltpu.make_async_copy(ref, ref, sem).wait()


def fill_window(info, qkv_ref, edge_ref, window, sems):
    core = info[1]
    first = pl.multiple_of(jnp.where(core == 1, 0, WINDOW_HALF + ROWS), 16)
    last = pl.multiple_of(jnp.where(core == 1, WINDOW_HALF + ROWS, 0), 16)
    copies = [
        pltpu.make_async_copy(edge_ref, window.at[pl.ds(first, WINDOW_HALF), :], sems.at[4])
    ]
    for part in range(2):
        for half in range(2):
            copies.append(
                pltpu.make_async_copy(
                    qkv_ref.at[:, pl.ds(HALF * half + 384 * (part + 1), 384)],
                    window.at[pl.ds(WINDOW_HALF, ROWS), pl.ds(WIDTH * part + 384 * half, 384)],
                    sems.at[2 * part + half],
                )
            )
    for copy in copies:
        copy.start()
    window[pl.ds(last, WINDOW_HALF), :] = jnp.zeros((WINDOW_HALF, 2 * WIDTH), BF16)
    for copy in copies:
        copy.wait()


def normalized(values):
    centred = values - jnp.mean(values, axis=-1, keepdims=True)
    spread = jnp.mean(centred * centred, axis=-1, keepdims=True)
    factor = lax.rsqrt(spread + 1e-05)
    return centred * factor, factor


def norm_backward(grad, unit, factor, gain):
    inner = grad * gain
    mean = jnp.mean(inner, axis=-1, keepdims=True)
    along = jnp.mean(inner * unit, axis=-1, keepdims=True)
    return factor * (inner - mean - unit * along)


def turned(values, cosine, sine):
    lane = lax.broadcasted_iota(jnp.int32, values.shape, 1)
    first = (lane & 32) == 0
    other = jnp.where(first, pltpu.roll(values, 96, 1), pltpu.roll(values, 32, 1))
    return values * cosine + other * sine


def both_heads(block):
    lane = lax.broadcasted_iota(jnp.int32, block.shape, 1)
    first = jnp.where(lane < HEAD_DIM, 1.0, 0.0).astype(block.dtype)
    second = jnp.where(lane < HEAD_DIM, 0.0, 1.0).astype(block.dtype)
    return jnp.concatenate([block * first, block * second], axis=0)


def head_lanes(rows):
    lane = lax.broadcasted_iota(jnp.int32, (LANES, LANES), 1)
    return jnp.where(lane < HEAD_DIM, rows[:LANES], rows[LANES:])


def qkv_kernel(order, pieces_of, info, x_ref, cos_ref, sin_ref, *refs):
    count_a, count_b = pieces_of
    order_a, order_b = order
    part_a, refs = refs[:count_a], refs[count_a:]
    part_b, refs = refs[:count_b], refs[count_b:]
    qkv_ref, normed_ref, gain_ref, edge_ref, weight, gains, sems = refs
    step = pl.program_id(0)
    rows = x_ref.shape[0]

    @pl.when(step == 0)
    def _():
        into = lambda offset: (weight, 0, HALF, offset)
        start_slots(info, part_a, order_a, [(0, FIRST_CUT, into(0), into(0))], sems)
        rest = HALF - FIRST_CUT
        start_slots(
            info,
            part_b,
            order_b,
            [
                (0, rest, into(FIRST_CUT), into(FIRST_CUT)),
                (rest, LANES, (gains, 1, 0, 0), None),
            ],
            sems,
        )
        wait_whole(weight, sems.at[0])
        wait_whole(gains, sems.at[1])
        row = lax.broadcasted_iota(jnp.int32, (16, LANES), 0)
        lane = lax.broadcasted_iota(jnp.int32, (16, LANES), 1)
        pick = jnp.where(row == lane, 1.0, 0.0).astype(BF16)
        gain_ref[...] = nt(pick, gains[...])[:8]

    unit, unused = normalized(x_ref[...].astype(F32))
    normed = (unit * gain_ref[0:1, :]).astype(BF16)
    normed_ref[...] = normed
    cosine, sine = cos_ref[...], sin_ref[...]
    for half in range(2):
        result = nn(normed, weight[:, HALF * half : HALF * (half + 1)])
        for tile in range(9):
            block = result[:, LANES * tile : LANES * (tile + 1)]
            if tile < 6:
                block = turned(block, cosine, sine)
            if tile < 3:
                block = block * (HEAD_DIM**-0.5)
            begin = HALF * half + LANES * tile
            qkv_ref[:, begin : begin + LANES] = block.astype(BF16)

    for core, at_step, begin in ((1, 0, 0), (0, ROWS // rows - 1, rows - WINDOW_HALF)):

        @pl.when((info[1] == core) & (step == at_step))
        def _():
            for part in range(2):
                for half in range(2):
                    source = HALF * half + 384 * (part + 1)
                    target = WIDTH * part + 384 * half
                    edge_ref[:, target : target + 384] = qkv_ref[
                        begin : begin + WINDOW_HALF, source : source + 384
                    ]


def attend_kernel(
    info, row_seg, col_seg, q_ref, qkv_ref, edge_ref, out_ref, probs_ref, window, sems
):
    step = pl.program_id(0)

    @pl.when(step == 0)
    def _():
        fill_window(info, qkv_ref, edge_ref, window, sems)

    start = pl.multiple_of(step * LANES, LANES)
    key_seg = col_seg[pl.ds(start, SPAN), :]
    key_at = lax.broadcasted_iota(jnp.int32, (SPAN, LANES), 0) - WINDOW_HALF
    query_at = lax.broadcasted_iota(jnp.int32, (SPAN, LANES), 1)
    near = jnp.abs(key_at - query_at) <= WINDOW_HALF
    allowed = (key_seg == row_seg[0]) & near
    bias = jnp.where(allowed, 0.0, -1e30)
    bias = jnp.concatenate([bias, bias], axis=1)
    for pair in range(PAIRS):
        half, tile = pair // 3, pair % 3
        begin = HALF * half + LANES * tile
        lanes = slice(LANES * pair, LANES * (pair + 1))
        queries = both_heads(q_ref[:, begin : begin + LANES])
        keys = window[pl.ds(start, SPAN), lanes]
        values = window[pl.ds(start, SPAN), WIDTH + LANES * pair : WIDTH + LANES * (pair + 1)]
        scores = nt(keys, queries) + bias
        weights = jnp.exp(scores - jnp.max(scores, axis=0, keepdims=True))
        total = jnp.sum(weights, axis=0, keepdims=True)
        probs = (weights * (1.0 / total)).astype(BF16)
        probs_ref[0, pair] = probs
        out_ref[:, lanes] = head_lanes(tn(probs, values)).astype(BF16)


def mlp_kernel(order, count, info, x_ref, att_ref, cot_ref, live_ref, gain_ref, *refs):
    order_in, order_down = order
    part_in, refs = refs[: count[0]], refs[count[0] :]
    part_down, refs = refs[: count[1]], refs[count[1] :]
    (
        out_ref,
        hidden_grad_ref,
        att_grad_ref,
        normed_ref,
        gated_ref,
        pre_grad_ref,
        low_grad_ref,
        out_grad_ref,
        gain_grad_ref,
        w_in,
        w_att,
        w_out,
        tail_own,
        tail_other,
        sems,
    ) = refs
    step = pl.program_id(0)

    @pl.when(step == 0)
    def _():
        into = (w_in, 0, HALF, 0)
        start_slots(info, part_in, order_in, [(0, HALF, into, into)], sems)
        att, out = (w_att, 1, 384, 0), (w_out, 2, UNITS, 0)
        start_slots(
            info,
            part_down,
            order_down,
            [
                (0, 384, att, att),
                (384, UNITS, out, out),
                (384 + UNITS, LANES, (tail_own, 3, 0, 0), (tail_other, 4, 0, 0)),
            ],
            sems,
        )
        wait_whole(w_att, sems.at[1])
        wait_whole(w_in, sems.at[0])
        wait_whole(w_out.at[:, pl.ds(0, 2 * UNITS)], sems.at[2])
        wait_whole(tail_own, sems.at[3])
        wait_whole(tail_other, sems.at[4])
        w_out[:, 2 * UNITS :] = tail_own[...] + tail_other[...]
        gain_grad_ref[...] = jnp.zeros_like(gain_grad_ref)

    gain = gain_ref[1:2, :]
    hidden = x_ref[...].astype(F32) + nt(att_ref[...], w_att[...])
    unit, factor = normalized(hidden)
    normed = (unit * gain).astype(BF16)
    normed_ref[...] = normed
    out_grad = cot_ref[...].astype(F32) * live_ref[...]
    out_grad_low = out_grad.astype(BF16)
    out_grad_ref[...] = out_grad_low
    pre = [nn(normed, w_in[:, HALF * half : HALF * (half + 1)]) for half in range(2)]
    tails = [part[:, 2 * UNITS :] for part in pre]
    lane = lax.broadcasted_iota(jnp.int32, tails[0].shape, 1)
    low = lane < HEAD_DIM
    gates = [part[:, :UNITS] for part in pre]
    gates.append(jnp.where(low, tails[0], pltpu.roll(tails[1], 64, 1)))
    ups = [part[:, UNITS : 2 * UNITS] for part in pre]
    ups.append(jnp.where(low, pltpu.roll(tails[0], 64, 1), tails[1]))
    for part, (gate, up) in enumerate(zip(gates, ups)):
        columns = slice(UNITS * part, UNITS * part + gate.shape[1])
        share = 0.5 + 0.5 * lax.erf(gate * (0.5**0.5))
        slope = share + gate * (jnp.exp(-0.5 * gate * gate) * 0.3989422804014327)
        curve = gate * share
        gated_ref[:, columns] = (curve * up).astype(BF16)
        grad = nn(out_grad_low, w_out[:, columns])
        gate_grad = (grad * up * slope).astype(BF16)
        up_grad = (grad * curve).astype(BF16)
        if part < 2:
            begin = HALF * part
            pre_grad_ref[:, begin : begin + UNITS] = gate_grad
            pre_grad_ref[:, begin + UNITS : begin + 2 * UNITS] = up_grad
        else:
            gate_grad = gate_grad.astype(F32)
            up_grad = up_grad.astype(F32)
            pre_grad_ref[:, 2 * UNITS : HALF] = jnp.where(
                low, gate_grad, pltpu.roll(up_grad, 64, 1)
            ).astype(BF16)
            pre_grad_ref[:, HALF + 2 * UNITS :] = jnp.where(
                low, pltpu.roll(gate_grad, 64, 1), up_grad
            ).astype(BF16)
    out_ref[...] = (hidden + nt(gated_ref[...], w_out[...])).astype(BF16)
    normed_grad = nt(pre_grad_ref[...], w_in[...])
    gain_grad_ref[0:1, :] += jnp.sum(normed_grad * unit, axis=0, keepdims=True)
    hidden_grad = out_grad + norm_backward(normed_grad, unit, factor, gain)
    hidden_grad_ref[...] = hidden_grad
    hidden_grad_low = hidden_grad.astype(BF16)
    low_grad_ref[...] = hidden_grad_low
    att_grad_ref[...] = nn(hidden_grad_low, w_att[...]).astype(BF16)


def weight_grad_kernel(lefts, cuts, orders, info, *refs):
    count = max(lefts) + 1
    left, refs = refs[:count], refs[count:]
    right, refs = refs[: len(lefts)], refs[len(lefts) :]
    outs, total = refs[:-1], refs[-1]
    begin = 0
    for which, ref in zip(lefts, right):
        width = ref.shape[1]
        total[:, begin : begin + width] = tn(left[which][...], ref[...]).astype(BF16)
        begin += width
    for out, (start, stop), order in zip(outs, cuts, orders):
        rows = out.shape[1]
        for slot in range(out.shape[0]):
            row = pl.multiple_of((info[0] ^ order[slot]) * rows, 16)
            out[slot] = total[pl.ds(row, rows), start:stop]


def attend_back_kernel(
    info,
    q_ref,
    probs_ref,
    grad_ref,
    cos_ref,
    sin_ref,
    qkv_ref,
    edge_ref,
    out_ref,
    edge_out_ref,
    window,
    key_grad,
    value_grad,
    sems,
):
    step = pl.program_id(0)

    @pl.when(step == 0)
    def _():
        fill_window(info, qkv_ref, edge_ref, window, sems)
        key_grad[...] = jnp.zeros_like(key_grad)
        value_grad[...] = jnp.zeros_like(value_grad)

    start = pl.multiple_of(step * LANES, LANES)
    span = pl.ds(start, SPAN)
    cosine, sine = cos_ref[pl.ds(start, LANES), :], sin_ref[pl.ds(start, LANES), :]
    for pair in range(PAIRS):
        half, tile = pair // 3, pair % 3
        begin = HALF * half + LANES * tile
        lanes = slice(LANES * pair, LANES * (pair + 1))
        queries = both_heads(q_ref[:, begin : begin + LANES])
        grads = both_heads(grad_ref[:, lanes])
        keys = window[span, lanes]
        values = window[span, WIDTH + LANES * pair : WIDTH + LANES * (pair + 1)]
        probs = probs_ref[0, pair]
        probs_wide = probs.astype(F32)
        probs_grad = nt(values, grads)
        weighted = probs_grad * probs_wide
        delta = jnp.sum(weighted, axis=0, keepdims=True)
        score_grad = (weighted - probs_wide * delta).astype(BF16)
        query_grad = head_lanes(tn(score_grad, keys)) * (HEAD_DIM**-0.5)
        out_ref[pl.ds(start, LANES), begin : begin + LANES] = turned(
            query_grad, cosine, -sine
        ).astype(BF16)
        key_grad[span, lanes] += nn(score_grad, queries)
        value_grad[span, lanes] += nn(probs, grads)

    @pl.when(step == ROWS // LANES - 1)
    def _():
        for pair in range(PAIRS):
            half, tile = pair // 3, pair % 3
            begin = HALF * half + LANES * tile
            lanes = slice(LANES * pair, LANES * (pair + 1))
            inside = slice(WINDOW_HALF, WINDOW_HALF + ROWS)
            out_ref[:, begin + 384 : begin + 384 + LANES] = turned(
                key_grad[inside, lanes], cos_ref[...], -sin_ref[...]
            ).astype(BF16)
            out_ref[:, begin + 768 : begin + 768 + LANES] = value_grad[inside, lanes].astype(BF16)
        row = pl.multiple_of(jnp.where(info[1] == 1, 0, WINDOW_HALF + ROWS), 16)
        edge_out_ref[:, :WIDTH] = key_grad[pl.ds(row, WINDOW_HALF), :].astype(BF16)
        edge_out_ref[:, WIDTH:] = value_grad[pl.ds(row, WINDOW_HALF), :].astype(BF16)


def edge_kernel(info, grad_ref, edge_ref, cos_ref, sin_ref, out_ref):
    out_ref[...] = grad_ref[...]
    for pair in range(PAIRS):
        half, tile = pair // 3, pair % 3
        begin = HALF * half + LANES * tile
        keys = turned(
            edge_ref[:, LANES * pair : LANES * (pair + 1)].astype(F32), cos_ref[...], -sin_ref[...]
        )
        values = edge_ref[:, WIDTH + LANES * pair : WIDTH + LANES * (pair + 1)].astype(F32)
        for offset, add in ((384, keys), (768, values)):
            at = slice(begin + offset, begin + offset + LANES)
            out_ref[:, at] = (grad_ref[:, at].astype(F32) + add).astype(BF16)


def input_grad_kernel(
    order, pieces_of, info, x_ref, grad_ref, hidden_grad_ref, gain_ref, *refs
):
    count_a, count_b = pieces_of
    order_a, order_b = order
    part_a, refs = refs[:count_a], refs[count_a:]
    part_b, refs = refs[:count_b], refs[count_b:]
    out_ref, gain_grad_ref, weight, sems = refs

    @pl.when(pl.program_id(0) == 0)
    def _():
        into = lambda offset: (weight, 0, HALF, offset)
        start_slots(info, part_a, order_a, [(0, FIRST_CUT, into(0), into(0))], sems)
        rest = (0, HALF - FIRST_CUT, into(FIRST_CUT), into(FIRST_CUT))
        start_slots(info, part_b, order_b, [rest], sems)
        gain_grad_ref[...] = jnp.zeros_like(gain_grad_ref)
        wait_whole(weight, sems.at[0])

    unit, factor = normalized(x_ref[...].astype(F32))
    normed_grad = nt(grad_ref[...], weight[...])
    gain_grad_ref[0:1, :] += jnp.sum(normed_grad * unit, axis=0, keepdims=True)
    out_ref[...] = hidden_grad_ref[...] + norm_backward(
        normed_grad, unit, factor, gain_ref[0:1, :]
    )


def shape_of(shape, dtype=BF16):
    return jax.ShapeDtypeStruct(shape, dtype)


def call(kernel, info, grid, ins, in_specs, outs, out_specs, scratch, flops, aliases=None):
    moved = sum(a.size * a.dtype.itemsize for a in list(ins) + list(outs))
    return pl.pallas_call(
        kernel,
        out_shape=outs,
        grid_spec=pltpu.PrefetchScalarGridSpec(
            num_scalar_prefetch=1,
            grid=grid,
            in_specs=in_specs,
            out_specs=out_specs,
            scratch_shapes=scratch,
        ),
        input_output_aliases=aliases or {},
        compiler_params=pltpu.CompilerParams(
            dimension_semantics=("arbitrary",), vmem_limit_bytes=VMEM
        ),
        cost_estimate=pl.CostEstimate(
            flops=int(flops), bytes_accessed=int(moved), transcendentals=0
        ),
    )(info, *ins)


def by_rows(rows, columns):
    return pl.BlockSpec((rows, columns), lambda i, s: (i, 0))


def full(*shape):
    return pl.BlockSpec(shape, lambda i, s: (0,) * len(shape))


ANYWHERE = pl.BlockSpec(memory_space=pl.ANY)


def weight_grads(info, lefts, jobs, cuts, orders, slots, send):
    in_specs = [full(ROWS, WIDTH) for unused in lefts]
    for unused, right, width, block in jobs:
        if block is None:
            in_specs.append(pl.BlockSpec((ROWS, width), lambda i, s: (0, s[1] ^ send)))
        else:
            in_specs.append(pl.BlockSpec((ROWS, width), lambda i, s, block=block: (0, block)))
    total = sum(job[2] for job in jobs)
    outs = [shape_of((slots, WIDTH // slots, stop - start)) for start, stop in cuts]
    which = tuple(job[0] for job in jobs)
    return call(
        lambda *refs: weight_grad_kernel(which, cuts, orders, *refs),
        info,
        (1,),
        list(lefts) + [job[1] for job in jobs],
        in_specs,
        outs,
        [full(*out.shape) for out in outs],
        [pltpu.VMEM((WIDTH, total), BF16)],
        2 * ROWS * WIDTH * total,
    )


def body(
    tokens,
    segment,
    norm_attn_gain,
    qkv_weight,
    attn_out_weight,
    norm_mlp_gain,
    in_weight,
    out_weight,
    cotangent,
):
    own_rows = norm_attn_gain.shape[0]
    core = lax.axis_index("tensor")
    place = lax.axis_index("dp") if by_exchange(own_rows) else 0
    info = jnp.stack([jnp.int32(place), core.astype(jnp.int32)])
    order = relative(own_rows, False)
    order_swapped = relative(own_rows, True)
    slots = len(order)

    gains = jnp.pad(jnp.stack([norm_attn_gain, norm_mlp_gain], axis=1), ((0, 0), (0, LANES - 2)))
    flat = qkv_weight.reshape(own_rows, HALF)
    part_a = gather_slots(flat[:, :FIRST_CUT], False)
    part_b = gather_slots(jnp.concatenate([flat[:, FIRST_CUT:], gains], axis=1), True)
    part_a = part_a + [swapped_cores(piece) for piece in part_a]
    part_b = part_b + [swapped_cores(piece) for piece in part_b]
    shard_in = jnp.concatenate(
        [
            in_weight[:, 0, :UNITS],
            in_weight[:, 1, :UNITS],
            in_weight[:, 0, UNITS:],
            in_weight[:, 1, UNITS:],
        ],
        axis=1,
    )
    turned_out = out_weight.T
    tail = turned_out[:, UNITS:]
    blank = jnp.zeros_like(tail)
    tail = jnp.where(
        core == 0,
        jnp.concatenate([tail, blank], axis=1),
        jnp.concatenate([blank, tail], axis=1),
    )
    shard_down = jnp.concatenate([attn_out_weight.T, turned_out[:, :UNITS], tail], axis=1)
    part_in = gather_slots(shard_in, False)
    part_down = gather_slots(shard_down, True)
    part_in = part_in + [swapped_cores(piece) for piece in part_in]
    part_down = part_down + [swapped_cores(piece) for piece in part_down]

    own_segment = lax.dynamic_slice_in_dim(segment, core * ROWS, ROWS, 0)
    slot = core * ROWS + jnp.arange(ROWS, dtype=jnp.int32)
    position = jnp.where(own_segment >= 0, slot - PAD_BLOCK * own_segment, 0)
    lane = jnp.arange(LANES, dtype=jnp.int32)
    exponent = (lane % 32).astype(F32) * (2.0 / HEAD_DIM)
    angle = position.astype(F32)[:, None] * jnp.power(10000.0, -exponent)[None, :]
    cosine = jnp.cos(angle)
    sine = jnp.sin(angle) * jnp.where((lane & 32) == 0, -1.0, 1.0)[None, :]
    seg_pad = jnp.pad(segment, (WINDOW_HALF, WINDOW_HALF), constant_values=-2)
    col_seg = lax.dynamic_slice_in_dim(seg_pad, core * ROWS, ROWS + 2 * WINDOW_HALF, 0)[:, None]
    row_seg = own_segment.reshape(ROWS // LANES, 1, LANES)
    live = (own_segment >= 0).astype(F32)[:, None]

    rows = 384
    steps = ROWS // rows
    pieces_of = (len(part_a), len(part_b))
    qkv, normed, gain_rows, edge = call(
        lambda *refs: qkv_kernel((order, order_swapped), pieces_of, *refs),
        info,
        (steps,),
        [tokens, cosine, sine, *part_a, *part_b],
        [by_rows(rows, WIDTH), by_rows(rows, LANES), by_rows(rows, LANES)]
        + [ANYWHERE] * sum(pieces_of),
        [
            shape_of((ROWS, 2 * HALF)),
            shape_of((ROWS, WIDTH)),
            shape_of((8, WIDTH), F32),
            shape_of((WINDOW_HALF, 2 * WIDTH)),
        ],
        [by_rows(rows, 2 * HALF), by_rows(rows, WIDTH), full(8, WIDTH), full(64, 2 * WIDTH)],
        [
            pltpu.VMEM((WIDTH, 2 * HALF), BF16),
            pltpu.VMEM((WIDTH, LANES), BF16),
            pltpu.SemaphoreType.DMA((2,)),
        ],
        2 * ROWS * WIDTH * 2 * HALF,
    )
    edge = swapped_cores(edge)

    blocks = ROWS // LANES
    window_shape = (ROWS + 2 * WINDOW_HALF, 2 * WIDTH)
    attended, probs = call(
        attend_kernel,
        info,
        (blocks,),
        [row_seg, col_seg, qkv, qkv, edge],
        [
            pl.BlockSpec((1, 1, LANES), lambda i, s: (i, 0, 0)),
            full(ROWS + 2 * WINDOW_HALF, 1),
            by_rows(LANES, 2 * HALF),
            ANYWHERE,
            ANYWHERE,
        ],
        [shape_of((ROWS, WIDTH)), shape_of((blocks, PAIRS, SPAN, SPAN))],
        [
            by_rows(LANES, WIDTH),
            pl.BlockSpec((1, PAIRS, SPAN, SPAN), lambda i, s: (i, 0, 0, 0)),
        ],
        [pltpu.VMEM(window_shape, BF16), pltpu.SemaphoreType.DMA((5,))],
        blocks * PAIRS * 2 * 2 * SPAN * SPAN * LANES,
    )

    (
        layer_out,
        hidden_grad,
        att_grad,
        normed_two,
        gated,
        pre_grad,
        hidden_grad_low,
        out_grad,
        gain_two_grad,
    ) = call(
        lambda *refs: mlp_kernel(
            (order, order_swapped), (len(part_in), len(part_down)), *refs
        ),
        info,
        (steps,),
        [tokens, attended, cotangent, live, gain_rows, *part_in, *part_down],
        [by_rows(rows, WIDTH)] * 3
        + [by_rows(rows, 1), full(8, WIDTH)]
        + [ANYWHERE] * (len(part_in) + len(part_down)),
        [
            shape_of((ROWS, WIDTH)),
            shape_of((ROWS, WIDTH), F32),
            shape_of((ROWS, WIDTH)),
            shape_of((ROWS, WIDTH)),
            shape_of((ROWS, HALF)),
            shape_of((ROWS, 2 * HALF)),
            shape_of((ROWS, WIDTH)),
            shape_of((ROWS, WIDTH)),
            shape_of((8, WIDTH), F32),
        ],
        [by_rows(rows, WIDTH)] * 4
        + [by_rows(rows, HALF), by_rows(rows, 2 * HALF)]
        + [by_rows(rows, WIDTH)] * 2
        + [full(8, WIDTH)],
        [
            pltpu.VMEM((WIDTH, 2 * HALF), BF16),
            pltpu.VMEM((WIDTH, WIDTH), BF16),
            pltpu.VMEM((WIDTH, HALF), BF16),
            pltpu.VMEM((WIDTH, LANES), BF16),
            pltpu.VMEM((WIDTH, LANES), BF16),
            pltpu.SemaphoreType.DMA((5,)),
        ],
        2 * ROWS * WIDTH * (4 * HALF + 2 * HALF + 2 * WIDTH),
    )

    early = (
        info,
        [normed_two, hidden_grad_low, out_grad],
        [
            (0, pre_grad, HALF, None),
            (1, attended, 384, None),
            (2, gated, UNITS, None),
            (2, gated, LANES, 2 * UNITS // LANES),
        ],
        [(0, HALF), (HALF, HALF + DOWN)],
        [order, order_swapped],
        slots,
    )
    send_in, send_down = weight_grads(*early, 1)
    keep_in, keep_down = weight_grads(*early, 0)
    owned_in = scatter_slots(keep_in, send_in, own_rows, False)
    owned_down = scatter_slots(keep_down, send_down, own_rows, True)

    qkv_grad, edge_grad = call(
        attend_back_kernel,
        info,
        (blocks,),
        [qkv, probs, att_grad, cosine, sine, qkv, edge],
        [
            by_rows(LANES, 2 * HALF),
            pl.BlockSpec((1, PAIRS, SPAN, SPAN), lambda i, s: (i, 0, 0, 0)),
            by_rows(LANES, WIDTH),
            full(ROWS, LANES),
            full(ROWS, LANES),
            ANYWHERE,
            ANYWHERE,
        ],
        [shape_of((ROWS, 2 * HALF)), shape_of((WINDOW_HALF, 2 * WIDTH))],
        [full(ROWS, 2 * HALF), full(WINDOW_HALF, 2 * WIDTH)],
        [
            pltpu.VMEM(window_shape, BF16),
            pltpu.VMEM((window_shape[0], WIDTH), F32),
            pltpu.VMEM((window_shape[0], WIDTH), F32),
            pltpu.SemaphoreType.DMA((5,)),
        ],
        blocks * PAIRS * 4 * 2 * SPAN * SPAN * LANES,
    )
    edge_grad = swapped_cores(edge_grad)
    at_edge = lambda i, s: ((1 - s[1]) * (ROWS // WINDOW_HALF - 1), 0)
    (qkv_grad,) = call(
        edge_kernel,
        info,
        (1,),
        [qkv_grad, edge_grad, cosine, sine],
        [
            pl.BlockSpec((WINDOW_HALF, 2 * HALF), at_edge),
            full(WINDOW_HALF, 2 * WIDTH),
            pl.BlockSpec((WINDOW_HALF, LANES), at_edge),
            pl.BlockSpec((WINDOW_HALF, LANES), at_edge),
        ],
        [shape_of((ROWS, 2 * HALF))],
        [pl.BlockSpec((WINDOW_HALF, 2 * HALF), at_edge)],
        [],
        0,
        {1: 0},
    )

    late = (
        info,
        [normed],
        [(0, qkv_grad, HALF, None)],
        [(0, FIRST_CUT), (FIRST_CUT, HALF)],
        [order, order_swapped],
        slots,
    )
    send_a, send_b = weight_grads(*late, 1)
    keep_a, keep_b = weight_grads(*late, 0)
    owned_a = scatter_slots(keep_a, send_a, own_rows, False)
    owned_b = scatter_slots(keep_b, send_b, own_rows, True)

    grad_tokens, gain_one_grad = call(
        lambda *refs: input_grad_kernel((order, order_swapped), pieces_of, *refs),
        info,
        (steps,),
        [tokens, qkv_grad, hidden_grad, gain_rows, *part_a, *part_b],
        [by_rows(rows, WIDTH), by_rows(rows, 2 * HALF), by_rows(rows, WIDTH), full(8, WIDTH)]
        + [ANYWHERE] * sum(pieces_of),
        [shape_of((ROWS, WIDTH), F32), shape_of((8, WIDTH), F32)],
        [by_rows(rows, WIDTH), full(8, WIDTH)],
        [pltpu.VMEM((WIDTH, 2 * HALF), BF16), pltpu.SemaphoreType.DMA((1,))],
        2 * ROWS * WIDTH * 2 * HALF,
    )
    owned_gain_one, owned_gain_two = scatter_gains(gain_one_grad[0], gain_two_grad[0])

    owned_qkv = jnp.concatenate([owned_a, owned_b], axis=1).reshape(own_rows, 3, HALF // 3)
    owned_in = jnp.stack(
        [
            jnp.concatenate([owned_in[:, :UNITS], owned_in[:, 2 * UNITS : -64]], axis=1),
            jnp.concatenate([owned_in[:, UNITS : 2 * UNITS], owned_in[:, -64:]], axis=1),
        ],
        axis=1,
    )
    owned_attn = owned_down[:, :384].T
    tail = jnp.where(core == 0, owned_down[:, -128:-64], owned_down[:, -64:])
    owned_out = jnp.concatenate([owned_down[:, 384 : 384 + UNITS], tail], axis=1).T
    return (
        layer_out,
        grad_tokens,
        owned_gain_one,
        owned_qkv,
        owned_attn,
        owned_gain_two,
        owned_in,
        owned_out,
    )


def solution(mesh):
    placed = (
        P(("dp", "tensor"), None),
        P("dp"),
        P("dp"),
        P("dp", None, "tensor"),
        P("tensor", "dp"),
        P("dp"),
        P("dp", None, "tensor"),
        P("tensor", "dp"),
        P(("dp", "tensor"), None),
    )
    return jax.shard_map(
        body,
        mesh=mesh,
        in_specs=placed,
        out_specs=(
            P(("dp", "tensor"), None),
            P(("dp", "tensor"), None),
            P("dp"),
            P("dp", None, "tensor"),
            P("tensor", "dp"),
            P("dp"),
            P("dp", None, "tensor"),
            P("tensor", "dp"),
        ),
        check_vma=False,
    )
```

time: 1020 us -> 343 us (0.34)
  waiting for transfers between devices: 332 us -> 120 us
  other arithmetic: 199 us -> 12.3 us
  blocking collectives: 175 us -> 0 us
  Pallas kernels: 0 us -> 138 us
  local copies, waits for them, and re-layouts: 151 us -> 14.1 us
  matrix products: 124 us -> 0 us
  starting transfers between devices: 10.5 us -> 53 us
  between operations: 16.5 us -> 1.42 us
    reduce_scatter x4 -> x0, waiting for transfers between devices: 316 us -> none  [the longest x1 153 us: body(): lax.psum_scatter(grad_weight_in, 'dp', scatter_dimension=0, tiled=True)]
    pallas_call x0 -> x10, Pallas kernels: none -> 138 us  [call(): pl.pallas_call(kernel, out_shape=outs, grid_spec=pltpu.PrefetchScalarGrid...]
    dot_general x18 -> x0, matrix products: 124 us -> none  [the longest x1 14.1 us: body(): jnp.einsum('rd,rcf->dcf', normed_two_low, grad_pre, preferred_element_typ...]
    ppermute x4 -> x51, waiting for transfers between devices: 0.01 us -> 120 us  [the longest x36 120 us: exchanged(): return lax.ppermute(block, 'dp', [(i, i ^ mask) for i in range(devices)])]
    all_gather x2 -> x0, blocking collectives: 94.7 us -> none  [the longest x1 49.8 us: body(): lax.all_gather(out_weight, 'dp', axis=1, tiled=True)]
    sub x2 -> x0, other arithmetic: 92.7 us -> none  [the longest x1 92.1 us: one_block(): grad_scores = (probs * (grad_probs - delta)).astype(jnp.bfloat16)]
    unnamed x2 -> x0, blocking collectives: 76.9 us -> none
    unnamed x150 -> x27, local copies, waits for them, and re-layouts: 52 us -> 3.03 us
  transfers between devices with their start and end apart: 18 -> 51, of which waited for: 4 -> 22; matrix products, arithmetic and copies ran while one was open for 41% -> 6% of each run, Pallas kernels for 0% -> 19%
where the time goes in v2:
time: 343 us; the launch traced here: 340 us
  Pallas kernels  138 us (40%)
  waiting for transfers between devices  120 us (35%)
  starting transfers between devices  53 us (15%)
  local copies, waits for them, and re-layouts  14.1 us (4%)
  other arithmetic  12.3 us (4%)
    pallas_call x10, Pallas kernels, call(): pl.pallas_call(kernel, out_shape=outs, grid_spec=pltpu.PrefetchScalarGrid...  138 us
    ppermute x36, waiting for transfers between devices, exchanged(): return lax.ppermute(block, 'dp', [(i, i ^ mask) for i in range(devices)])  120 us
    ppermute x36, starting transfers between devices, exchanged(): return lax.ppermute(block, 'dp', [(i, i ^ mask) for i in range(devices)])  49.3 us
  transfers between devices with their start and end apart: 51, of which 22 were waited for; matrix products, arithmetic and copies ran while one was open for 6% of the time, Pallas kernels for 19%

profile of v2, /device:TPU:0, one launch (start us, length us, event | category | flops | bytes accessed | tf_op | source)
XLA Modules:
  0.0 339.5 jit_solution(4823956138389154714)
XLA Ops:
  18.8 12.4 %collective-permute-done.14 = bf16[2,48,1152]{2,1,0:T(8,128)(2,1)S(1)} collective-permute-done((bf16[2,48,1152]{2,1,0:T(8,128)(2,1)S(1)}, bf16[2,48,1152]{2,1,0:T(8,128)(2,1)S(1)}, u32[]{:S(2)}, u32[]{:S(2)}) %collective-permute-start.14) | collective-permute-done | bytes 221216 | tf_op jit(solution)/shard_map/ppermute | solution.py:33
  49.6 5.6 %collective-permute-done.21 = bf16[4,48,1024]{2,1,0:T(8,128)(2,1)} collective-permute-done((bf16[4,48,1024]{2,1,0:T(8,128)(2,1)S(1)}, bf16[4,48,1024]{2,1,0:T(8,128)(2,1)}, u32[]{:S(2)}, u32[]{:S(2)}) %collective-permute-start.21) | collective-permute-done | bytes 393248 | tf_op jit(solution)/shard_map/ppermute | solution.py:33
  59.1 22.8 %collective-permute-done.3.refs_5_.refs_6_ = bf16[8,48,640]{2,1,0:T(8,128)(2,1)} collective-permute-done((bf16[8,48,640]{2,1,0:T(8,128)(2,1)S(1)}, bf16[8,48,640]{2,1,0:T(8,128)(2,1)}, u32[]{:S(2)}, u32[]{:S(2)}) %collective-permute-start.3) | collective-permute-done | bytes 491552 | tf_op jit(solution)/shard_map/ppermute | solution.py:33
  83.3 3.8 %fusion.2 = (f32[1152,128]{1,0:T(8,128)}, f32[1152,128]{1,0:T(8,128)}) fusion(f32[128]{0:T(128)S(1)} %get-tuple-element.124, f32[128]{0:T(128)S(1)} %get-tuple-element.125, f32[1152]{0:T(1024)S(1)} %select_convert_fusion), kind=kLoop, calls=%fused_computation.18 | loop fusion | flops 294912 | bytes 1185280 | tf_op jit(solution)/shard_map/mul | solution.py:621
  88.2 11.7 %shard_map.152 = (bf16[1152,2304]{1,0:T(8,128)(2,1)}, bf16[1152,768]{1,0:T(8,128)(2,1)}, f32[8,768]{1,0:T(8,128)}, bf16[64,1536]{1,0:T(8,128)(2,1)}) custom-call(s32[2]{0:T(128)} %pad_add_fusion.1.refs_0_.info, bf16[1152,768]{1,0:T(8,128)(2,1)} %refs_1_.5, f32[1152,128]{1,0:T(8,128)} %get-tuple-element.121.refs_2_.cos_ref, ...), custom_call_target="tpu_custom_call" | custom-call | flops 4076863488 | bytes 14180352 | tf_op jit(solution)/shard_map/pallas_call | solution.py:512
  103.6 16.3 %shard_map.153 = (bf16[1152,768]{1,0:T(8,128)(2,1)}, bf16[9,6,256,256]{3,2,1,0:T(8,128)(2,1)}) custom-call(s32[2]{0:T(128)} %pad_add_fusion.1.refs_0_.info, s32[9,1,128]{2,1,0:T(1,128)} %reshape.54.row_seg, s32[1280,1]{1,0:T(8,128)} %broadcast_in_dim.44.col_seg, bf16[1152,2304]{1,0:T(8,128)(2,1)} %get-tuple-element.35.q_ref.qkv_ref, ...), custom_call_target="tpu_custom_call" | custom-call | flops 1811939328 | bytes 19670528 | tf_op jit(solution)/shard_map/pallas_call | solution.py:512
  120.0 28.9 %shard_map.154 = (bf16[1152,768]{1,0:T(8,128)(2,1)}, f32[1152,768]{1,0:T(8,128)}, bf16[1152,768]{1,0:T(8,128)(2,1)}, bf16[1152,768]{1,0:T(8,128)(2,1)}, bf16[115...) custom-call(s32[2]{0:T(128)} %pad_add_fusion.1.refs_0_.info, ...), custom_call_target="tpu_custom_call" | custom-call | flops 14948499456 | bytes 32395776 | tf_op jit(solution)/shard_map/pallas_call | solution.py:512
  148.8 28.8 %shard_map.155 = (bf16[1152,2304]{1,0:T(8,128)(2,1)}, bf16[64,1536]{1,0:T(8,128)(2,1)}) custom-call(s32[2]{0:T(128)} %pad_add_fusion.1.refs_0_.info, bf16[1152,2304]{1,0:T(8,128)(2,1)} %get-tuple-element.35.q_ref.qkv_ref, bf16[9,6,256,256]{3,2,1,0:T(8,128)(2,1)} %get-tuple-element.40.probs_ref, bf16[1152,768]{1,0:T(8,128)(2,1)} %get-tuple-element.41.grad_ref, ...), custom_call_target="tpu_custom_call" | custom-call | flops 3623878656 | bytes 26345472 | tf_op jit(solution)/shard_map/pallas_call | solution.py:512
  182.7 12.7 %shard_map.157 = (f32[1152,768]{1,0:T(8,128)}, f32[8,768]{1,0:T(8,128)}) custom-call(s32[2]{0:T(128)} %pad_add_fusion.1.refs_0_.info, bf16[1152,768]{1,0:T(8,128)(2,1)} %refs_1_.5, bf16[1152,2304]{1,0:T(8,128)(2,1)} %shard_map.156.refs_2_, f32[1152,768]{1,0:T(8,128)} %get-tuple-element.44.refs_3_, f32[8,768]{1,0:T(8,128)} %get-tuple-element.38.refs_5_.refs_4_, ...), custom_call_target="tpu_custom_call" | custom-call | flops 4076863488 | bytes 18137088 | tf_op jit(solution)/shard_map/pallas_call | solution.py:512
  196.6 11.6 %shard_map.160 = (bf16[16,48,1152]{2,1,0:T(8,128)(2,1)}, bf16[16,48,1024]{2,1,0:T(8,128)(2,1)}) custom-call(s32[2]{0:T(128)} %pad_add_fusion.1.refs_0_.info, bf16[1152,768]{1,0:T(8,128)(2,1)} %get-tuple-element.53.refs_1_, bf16[1152,768]{1,0:T(8,128)(2,1)} %get-tuple-element.54.refs_2_, bf16[1152,768]{1,0:T(8,128)(2,1)} %get-tuple-element.55.refs_3_, ...), custom_call_target="tpu_custom_call" | custom-call | flops 3850371072 | bytes 21037056 | tf_op jit(solution)/shard_map/pallas_call | solution.py:512
  209.9 11.5 %shard_map.161 = (bf16[16,48,1152]{2,1,0:T(8,128)(2,1)}, bf16[16,48,1024]{2,1,0:T(8,128)(2,1)}) custom-call(s32[2]{0:T(128)} %pad_add_fusion.1.refs_0_.info, bf16[1152,768]{1,0:T(8,128)(2,1)} %get-tuple-element.53.refs_1_, bf16[1152,768]{1,0:T(8,128)(2,1)} %get-tuple-element.54.refs_2_, bf16[1152,768]{1,0:T(8,128)(2,1)} %get-tuple-element.55.refs_3_, ...), custom_call_target="tpu_custom_call" | custom-call | flops 3850371072 | bytes 21037056 | tf_op jit(solution)/shard_map/pallas_call | solution.py:512
  223.6 7.0 %shard_map.159 = (bf16[16,48,640]{2,1,0:T(8,128)(2,1)}, bf16[16,48,512]{2,1,0:T(8,128)(2,1)}) custom-call(s32[2]{0:T(128)} %pad_add_fusion.1.refs_0_.info, bf16[1152,768]{1,0:T(8,128)(2,1)} %get-tuple-element.48.refs_1_, bf16[1152,2304]{1,0:T(8,128)(2,1)} %shard_map.156.refs_2_), custom_call_target="tpu_custom_call" | custom-call | flops 2038431744 | bytes 8847360 | tf_op jit(solution)/shard_map/pallas_call | solution.py:512
  231.1 7.2 %shard_map.158 = (bf16[16,48,640]{2,1,0:T(8,128)(2,1)}, bf16[16,48,512]{2,1,0:T(8,128)(2,1)}) custom-call(s32[2]{0:T(128)} %pad_add_fusion.1.refs_0_.info, bf16[1152,768]{1,0:T(8,128)(2,1)} %get-tuple-element.48.refs_1_, bf16[1152,2304]{1,0:T(8,128)(2,1)} %shard_map.156.refs_2_), custom_call_target="tpu_custom_call" | custom-call | flops 2038431744 | bytes 8847360 | tf_op jit(solution)/shard_map/pallas_call | solution.py:512
  238.4 5.7 %collective-permute-start.30 = (f32[1,1,1,1,8,128]{5,4,3,2,1,0:T(8,128)S(1)}, f32[1,1,1,1,8,128]{5,4,3,2,1,0:T(8,128)S(1)}, u32[]{:S(2)}, u32[]{:S(2)}) collective-permute-start(f32[1,1,1,1,8,128]{5,4,3,2,1,0:T(8,128)S(1)} %constant_dynamic-slice_fusion), channel_id=1, source_target_pairs={{0,8},{2,10},{4,12},{6,14},{8,0},{10,2},{12,4},{14,6},{16,24},{18,... | collective-permute-start | bytes 12296 | tf_op jit(solution)/shard_map/ppermute | solution.py:33
  246.9 9.1 %collective-permute-done.37 = bf16[8,48,512]{2,1,0:T(8,128)(2,1)S(1)} collective-permute-done((bf16[8,48,512]{2,1,0:T(8,128)(2,1)S(1)}, bf16[8,48,512]{2,1,0:T(8,128)(2,1)S(1)}, u32[]{:S(2)}, u32[]{:S(2)}) %collective-permute-start.37) | collective-permute-done | bytes 393248 | tf_op jit(solution)/shard_map/ppermute | solution.py:33
  257.2 5.6 %collective-permute-done.38 = bf16[4,48,512]{2,1,0:T(8,128)(2,1)S(1)} collective-permute-done((bf16[4,48,512]{2,1,0:T(8,128)(2,1)S(1)}, bf16[4,48,512]{2,1,0:T(8,128)(2,1)S(1)}, u32[]{:S(2)}, u32[]{:S(2)}) %collective-permute-start.38) | collective-permute-done | bytes 196640 | tf_op jit(solution)/shard_map/ppermute | solution.py:33
  275.1 4.4 %collective-permute-done.34 = bf16[2,48,640]{2,1,0:T(8,128)(2,1)S(1)} collective-permute-done((bf16[2,48,640]{2,1,0:T(8,128)(2,1)S(1)}, bf16[2,48,640]{2,1,0:T(8,128)(2,1)S(1)}, u32[]{:S(2)}, u32[]{:S(2)}) %collective-permute-start.34) | collective-permute-done | bytes 122912 | tf_op jit(solution)/shard_map/ppermute | solution.py:33
  280.1 6.8 %collective-permute-done.42 = bf16[8,48,1024]{2,1,0:T(8,128)(2,1)S(1)} collective-permute-done((bf16[8,48,1024]{2,1,0:T(8,128)(2,1)S(1)}, bf16[8,48,1024]{2,1,0:T(8,128)(2,1)S(1)}, u32[]{:S(2)}, u32[]{:S(2)}) %collective-permute-start.42) | collective-permute-done | bytes 786464 | tf_op jit(solution)/shard_map/ppermute | solution.py:33
  289.7 9.5 %collective-permute-done.43 = bf16[4,48,1024]{2,1,0:T(8,128)(2,1)S(1)} collective-permute-done((bf16[4,48,1024]{2,1,0:T(8,128)(2,1)S(1)}, bf16[4,48,1024]{2,1,0:T(8,128)(2,1)S(1)}, u32[]{:S(2)}, u32[]{:S(2)}) %collective-permute-start.43) | collective-permute-done | bytes 393248 | tf_op jit(solution)/shard_map/ppermute | solution.py:33
  302.6 5.4 %collective-permute-done.44 = bf16[2,48,1024]{2,1,0:T(8,128)(2,1)S(1)} collective-permute-done((bf16[2,48,1024]{2,1,0:T(8,128)(2,1)S(1)}, bf16[2,48,1024]{2,1,0:T(8,128)(2,1)S(1)}, u32[]{:S(2)}, u32[]{:S(2)}) %collective-permute-start.44) | collective-permute-done | bytes 196640 | tf_op jit(solution)/shard_map/ppermute | solution.py:33
  308.2 6.7 %collective-permute-done.47 = bf16[8,48,1152]{2,1,0:T(8,128)(2,1)S(1)} collective-permute-done((bf16[8,48,1152]{2,1,0:T(8,128)(2,1)S(1)}, bf16[8,48,1152]{2,1,0:T(8,128)(2,1)S(1)}, u32[]{:S(2)}, u32[]{:S(2)}) %collective-permute-start.47) | collective-permute-done | bytes 884768 | tf_op jit(solution)/shard_map/ppermute | solution.py:33
  316.5 7.5 %collective-permute-done.48 = bf16[4,48,1152]{2,1,0:T(8,128)(2,1)S(1)} collective-permute-done((bf16[4,48,1152]{2,1,0:T(8,128)(2,1)S(1)}, bf16[4,48,1152]{2,1,0:T(8,128)(2,1)S(1)}, u32[]{:S(2)}, u32[]{:S(2)}) %collective-permute-start.48) | collective-permute-done | bytes 442400 | tf_op jit(solution)/shard_map/ppermute | solution.py:33
  326.6 6.8 %collective-permute-done.49 = bf16[2,48,1152]{2,1,0:T(8,128)(2,1)S(1)} collective-permute-done((bf16[2,48,1152]{2,1,0:T(8,128)(2,1)S(1)}, bf16[2,48,1152]{2,1,0:T(8,128)(2,1)S(1)}, u32[]{:S(2)}, u32[]{:S(2)}) %collective-permute-start.49) | collective-permute-done | bytes 221216 | tf_op jit(solution)/shard_map/ppermute | solution.py:33
  334.2 4.1 %collective-permute-done.50 = bf16[1,48,1152]{2,1,0:T(8,128)(2,1)S(1)} collective-permute-done((bf16[1,48,1152]{2,1,0:T(8,128)(2,1)S(1)}, bf16[1,48,1152]{2,1,0:T(8,128)(2,1)S(1)}, u32[]{:S(2)}, u32[]{:S(2)}) %collective-permute-start.50) | collective-permute-done | bytes 110624 | tf_op jit(solution)/shard_map/ppermute | solution.py:33
  (198 shorter events, 86.1 us)
Async XLA Ops:
  2.4 13.3 %collective-permute-start.6 = (bf16[1,48,640]{2,1,0:T(8,128)(2,1)S(1)}, bf16[1,48,640]{2,1,0:T(8,128)(2,1)S(1)}, u32[]{:S(2)}, u32[]{:S(2)}) collective-permute-start(bf16[1,48,640]{2,1,0:T(8,128)(2,1)S(1)} %fusion.23), channel_id=1, source_target_pairs={{0,8},{2,10},{4,12},{6,14},{8,0},{10,2},{12,4},{14,6},{16,24},{18,... | collective-permute-start | bytes 184328 | tf_op jit(solution)/shard_map/ppermute | solution.py:33
  11.3 21.5 %collective-permute-start.19 = (bf16[1,48,1024]{2,1,0:T(8,128)(2,1)S(1)}, bf16[1,48,1024]{2,1,0:T(8,128)(2,1)S(1)}, u32[]{:S(2)}, u32[]{:S(2)}) collective-permute-start(bf16[1,48,1024]{2,1,0:T(8,128)(2,1)S(1)} %maximum_bitcast_fusion.3), channel_id=1, source_target_pairs={{0,8},{2,10},{4,12},{6,14},{8,0},{10,2},{12,4},{14,6},{16,24},{18,... | collective-permute-start | bytes 294920 | tf_op jit(solution)/shard_map/ppermute | solution.py:33
  13.1 18.1 %collective-permute-start.14 = (bf16[2,48,1152]{2,1,0:T(8,128)(2,1)S(1)}, bf16[2,48,1152]{2,1,0:T(8,128)(2,1)S(1)}, u32[]{:S(2)}, u32[]{:S(2)}) collective-permute-start(bf16[2,48,1152]{2,1,0:T(8,128)(2,1)S(1)} %pad_maximum_fusion.9), channel_id=1, source_target_pairs={{0,16},{2,18},{4,20},{6,22},{8,24},{10,26},{12,28},{14,30},{16,0},... | collective-permute-start | bytes 663560 | tf_op jit(solution)/shard_map/ppermute | solution.py:33
  15.7 18.1 %collective-permute-start.7 = (bf16[2,48,640]{2,1,0:T(8,128)(2,1)S(1)}, bf16[2,48,640]{2,1,0:T(8,128)(2,1)S(1)}, u32[]{:S(2)}, u32[]{:S(2)}) collective-permute-start(bf16[2,48,640]{2,1,0:T(8,128)(2,1)S(1)} %pad_maximum_fusion.13), channel_id=1, source_target_pairs={{0,16},{2,18},{4,20},{6,22},{8,24},{10,26},{12,28},{14,30},{16,0},... | collective-permute-start | bytes 368648 | tf_op jit(solution)/shard_map/ppermute | solution.py:33
  16.2 22.4 %collective-permute-start.1 = (bf16[2,48,640]{2,1,0:T(8,128)(2,1)S(1)}, bf16[2,48,640]{2,1,0:T(8,128)(2,1)S(1)}, u32[]{:S(2)}, u32[]{:S(2)}) collective-permute-start(bf16[2,48,640]{2,1,0:T(8,128)(2,1)S(1)} %pad_maximum_fusion.12), channel_id=1, source_target_pairs={{0,16},{2,18},{4,20},{6,22},{8,24},{10,26},{12,28},{14,30},{16,0},... | collective-permute-start | bytes 368648 | tf_op jit(solution)/shard_map/ppermute | solution.py:33
  31.2 13.4 %collective-permute-start.15 = (bf16[4,48,1152]{2,1,0:T(8,128)(2,1)S(1)}, bf16[4,48,1152]{2,1,0:T(8,128)(2,1)S(1)}, u32[]{:S(2)}, u32[]{:S(2)}) collective-permute-start(bf16[4,48,1152]{2,1,0:T(8,128)(2,1)S(1)} %pad_maximum_fusion.4), channel_id=1, source_target_pairs={{0,4},{2,6},{4,0},{6,2},{8,12},{10,14},{12,8},{14,10},{16,20},{18,... | collective-permute-start | bytes 1327112 | tf_op jit(solution)/shard_map/ppermute | solution.py:33
  43.0 12.2 %collective-permute-start.21 = (bf16[4,48,1024]{2,1,0:T(8,128)(2,1)S(1)}, bf16[4,48,1024]{2,1,0:T(8,128)(2,1)}, u32[]{:S(2)}, u32[]{:S(2)}) collective-permute-start(bf16[4,48,1024]{2,1,0:T(8,128)(2,1)S(1)} %pad_maximum_fusion.5), channel_id=1, source_target_pairs={{0,2},{2,0},{4,6},{6,4},{8,10},{10,8},{12,14},{14,12},{16,18},{18,... | collective-permute-start | bytes 1179656 | tf_op jit(solution)/shard_map/ppermute | solution.py:33
  44.8 37.8 %collective-permute-start.16 = (bf16[8,48,1152]{2,1,0:T(8,128)(2,1)S(1)}, bf16[8,48,1152]{2,1,0:T(8,128)(2,1)}, u32[]{:S(2)}, u32[]{:S(2)}) collective-permute-start(bf16[8,48,1152]{2,1,0:T(8,128)(2,1)S(1)} %pad_maximum_fusion.refs_6_), channel_id=1, source_target_pairs={{0,2},{2,0},{4,6},{6,4},{8,10},{10,8},{12,14},{14,12},{16,18},{18,... | collective-permute-start | bytes 2654216 | tf_op jit(solution)/shard_map/ppermute | solution.py:33
  47.0 34.9 %collective-permute-start.10 = (bf16[8,48,640]{2,1,0:T(8,128)(2,1)S(1)}, bf16[8,48,640]{2,1,0:T(8,128)(2,1)S(1)}, u32[]{:S(2)}, u32[]{:S(2)}) collective-permute-start(bf16[8,48,640]{2,1,0:T(8,128)(2,1)S(1)} %pad_maximum_fusion.3.refs_8_.refs_9_), channel_id=1, source_target_pairs={{0,1},{1,0},{2,3},{3,2},{4,5},{5,4},{6,7},{7,6},{8,9},{9,8},{10,11... | collective-permute-start | bytes 1474568 | tf_op jit(solution)/shard_map/ppermute | solution.py:37
  48.2 33.8 %collective-permute-start.3 = (bf16[8,48,640]{2,1,0:T(8,128)(2,1)S(1)}, bf16[8,48,640]{2,1,0:T(8,128)(2,1)}, u32[]{:S(2)}, u32[]{:S(2)}) collective-permute-start(bf16[8,48,640]{2,1,0:T(8,128)(2,1)S(1)} %pad_maximum_fusion.2.refs_4_.refs_5_), channel_id=1, source_target_pairs={{0,2},{2,0},{4,6},{6,4},{8,10},{10,8},{12,14},{14,12},{16,18},{18,... | collective-permute-start | bytes 1474568 | tf_op jit(solution)/shard_map/ppermute | solution.py:33
  55.3 27.2 %collective-permute-start.4 = (bf16[8,48,640]{2,1,0:T(8,128)(2,1)S(1)}, bf16[8,48,640]{2,1,0:T(8,128)(2,1)S(1)}, u32[]{:S(2)}, u32[]{:S(2)}) collective-permute-start(bf16[8,48,640]{2,1,0:T(8,128)(2,1)S(1)} %pad_maximum_fusion.2.refs_4_.refs_5_), channel_id=1, source_target_pairs={{0,1},{1,0},{2,3},{3,2},{4,5},{5,4},{6,7},{7,6},{8,9},{9,8},{10,11... | collective-permute-start | bytes 1474568 | tf_op jit(solution)/shard_map/ppermute | solution.py:37
  57.1 30.2 %collective-permute-start.22 = (bf16[8,48,1024]{2,1,0:T(8,128)(2,1)S(1)}, bf16[8,48,1024]{2,1,0:T(8,128)(2,1)}, u32[]{:S(2)}, u32[]{:S(2)}) collective-permute-start(bf16[8,48,1024]{2,1,0:T(8,128)(2,1)S(1)} %pad_maximum_fusion.1.refs_10_), channel_id=1, source_target_pairs={{0,4},{2,6},{4,0},{6,2},{8,12},{10,14},{12,8},{14,10},{16,20},{18,... | collective-permute-start | bytes 2359304 | tf_op jit(solution)/shard_map/ppermute | solution.py:33
  82.0 38.0 %collective-permute-start.17 = (bf16[8,48,1152]{2,1,0:T(8,128)(2,1)S(1)}, bf16[8,48,1152]{2,1,0:T(8,128)(2,1)}, u32[]{:S(2)}, u32[]{:S(2)}) collective-permute-start(bf16[8,48,1152]{2,1,0:T(8,128)(2,1)S(1)} %pad_maximum_fusion.refs_6_), channel_id=1, source_target_pairs={{0,1},{1,0},{2,3},{3,2},{4,5},{5,4},{6,7},{7,6},{8,9},{9,8},{10,11... | collective-permute-start | bytes 2654216 | tf_op jit(solution)/shard_map/ppermute | solution.py:37
  82.8 37.2 %collective-permute-start.18 = (bf16[8,48,1152]{2,1,0:T(8,128)(2,1)}, bf16[8,48,1152]{2,1,0:T(8,128)(2,1)}, u32[]{:S(2)}, u32[]{:S(2)}) collective-permute-start(bf16[8,48,1152]{2,1,0:T(8,128)(2,1)} %collective-permute-done.16.refs_7_), channel_id=1, source_target_pairs={{0,1},{1,0},{2,3},{3,2},{4,5},{5,4},{6,7},{7,6},{8,9},{9,8},{10,11... | collective-permute-start | bytes 2654216 | tf_op jit(solution)/shard_map/ppermute | solution.py:37
  87.0 32.9 %collective-permute-start.23 = (bf16[8,48,1024]{2,1,0:T(8,128)(2,1)S(1)}, bf16[8,48,1024]{2,1,0:T(8,128)(2,1)}, u32[]{:S(2)}, u32[]{:S(2)}) collective-permute-start(bf16[8,48,1024]{2,1,0:T(8,128)(2,1)S(1)} %pad_maximum_fusion.1.refs_10_), channel_id=1, source_target_pairs={{0,1},{1,0},{2,3},{3,2},{4,5},{5,4},{6,7},{7,6},{8,9},{9,8},{10,11... | collective-permute-start | bytes 2359304 | tf_op jit(solution)/shard_map/ppermute | solution.py:37
  87.3 32.7 %collective-permute-start.24 = (bf16[8,48,1024]{2,1,0:T(8,128)(2,1)}, bf16[8,48,1024]{2,1,0:T(8,128)(2,1)}, u32[]{:S(2)}, u32[]{:S(2)}) collective-permute-start(bf16[8,48,1024]{2,1,0:T(8,128)(2,1)} %collective-permute-done.22.refs_11_), channel_id=1, source_target_pairs={{0,1},{1,0},{2,3},{3,2},{4,5},{5,4},{6,7},{7,6},{8,9},{9,8},{10,11... | collective-permute-start | bytes 2359304 | tf_op jit(solution)/shard_map/ppermute | solution.py:37
  208.2 13.7 %collective-permute-start.27 = (f32[2,2,2,1,8,128]{5,4,3,2,1,0:T(8,128)S(1)}, f32[2,2,2,1,8,128]{5,4,3,2,1,0:T(8,128)S(1)}, u32[]{:S(2)}, u32[]{:S(2)}) collective-permute-start(f32[2,2,2,1,8,128]{5,4,3,2,1,0:T(8,128)S(1)} %constant_dynamic-slice_fusion.3), channel_id=1, source_target_pairs={{0,2},{2,0},{4,6},{6,4},{8,10},{10,8},{12,14},{14,12},{16,18},{18,... | collective-permute-start | bytes 98312 | tf_op jit(solution)/shard_map/ppermute | solution.py:33
  221.4 43.6 %collective-permute-start.41 = (bf16[16,48,1024]{2,1,0:T(8,128)(2,1)}, bf16[16,48,1024]{2,1,0:T(8,128)(2,1)S(1)}, u32[]{:S(2)}, u32[]{:S(2)}) collective-permute-start(bf16[16,48,1024]{2,1,0:T(8,128)(2,1)} %get-tuple-element.59), channel_id=1, source_target_pairs={{0,1},{1,0},{2,3},{3,2},{4,5},{5,4},{6,7},{7,6},{8,9},{9,8},{10,11... | collective-permute-start | bytes 4718600 | tf_op jit(solution)/shard_map/ppermute | solution.py:37
  221.4 66.3 %collective-permute-start.46 = (bf16[16,48,1152]{2,1,0:T(8,128)(2,1)}, bf16[16,48,1152]{2,1,0:T(8,128)(2,1)S(1)}, u32[]{:S(2)}, u32[]{:S(2)}) collective-permute-start(bf16[16,48,1152]{2,1,0:T(8,128)(2,1)} %get-tuple-element.61), channel_id=1, source_target_pairs={{0,1},{1,0},{2,3},{3,2},{4,5},{5,4},{6,7},{7,6},{8,9},{9,8},{10,11... | collective-permute-start | bytes 5308424 | tf_op jit(solution)/shard_map/ppermute | solution.py:37
  230.5 15.5 %collective-permute-start.31 = (bf16[16,48,640]{2,1,0:T(8,128)(2,1)}, bf16[16,48,640]{2,1,0:T(8,128)(2,1)S(1)}, u32[]{:S(2)}, u32[]{:S(2)}) collective-permute-start(bf16[16,48,640]{2,1,0:T(8,128)(2,1)} %get-tuple-element.50), channel_id=1, source_target_pairs={{0,1},{1,0},{2,3},{3,2},{4,5},{5,4},{6,7},{7,6},{8,9},{9,8},{10,11... | collective-permute-start | bytes 2949128 | tf_op jit(solution)/shard_map/ppermute | solution.py:37
  230.5 13.6 %collective-permute-start.36 = (bf16[16,48,512]{2,1,0:T(8,128)(2,1)}, bf16[16,48,512]{2,1,0:T(8,128)(2,1)S(1)}, u32[]{:S(2)}, u32[]{:S(2)}) collective-permute-start(bf16[16,48,512]{2,1,0:T(8,128)(2,1)} %get-tuple-element.52), channel_id=1, source_target_pairs={{0,1},{1,0},{2,3},{3,2},{4,5},{5,4},{6,7},{7,6},{8,9},{9,8},{10,11... | collective-permute-start | bytes 2359304 | tf_op jit(solution)/shard_map/ppermute | solution.py:37
  246.3 17.0 %collective-permute-start.32 = (bf16[8,48,640]{2,1,0:T(8,128)(2,1)S(1)}, bf16[8,48,640]{2,1,0:T(8,128)(2,1)S(1)}, u32[]{:S(2)}, u32[]{:S(2)}) collective-permute-start(bf16[8,48,640]{2,1,0:T(8,128)(2,1)S(1)} %get-tuple-element.96), channel_id=1, source_target_pairs={{0,2},{2,0},{4,6},{6,4},{8,10},{10,8},{12,14},{14,12},{16,18},{18,... | collective-permute-start | bytes 1474568 | tf_op jit(solution)/shard_map/ppermute | solution.py:33
  265.6 21.2 %collective-permute-start.42 = (bf16[8,48,1024]{2,1,0:T(8,128)(2,1)S(1)}, bf16[8,48,1024]{2,1,0:T(8,128)(2,1)S(1)}, u32[]{:S(2)}, u32[]{:S(2)}) collective-permute-start(bf16[8,48,1024]{2,1,0:T(8,128)(2,1)S(1)} %get-tuple-element.90), channel_id=1, source_target_pairs={{0,4},{2,6},{4,0},{6,2},{8,12},{10,14},{12,8},{14,10},{16,20},{18,... | collective-permute-start | bytes 2359304 | tf_op jit(solution)/shard_map/ppermute | solution.py:33
  288.7 26.1 %collective-permute-start.47 = (bf16[8,48,1152]{2,1,0:T(8,128)(2,1)S(1)}, bf16[8,48,1152]{2,1,0:T(8,128)(2,1)S(1)}, u32[]{:S(2)}, u32[]{:S(2)}) collective-permute-start(bf16[8,48,1152]{2,1,0:T(8,128)(2,1)S(1)} %get-tuple-element.88), channel_id=1, source_target_pairs={{0,2},{2,0},{4,6},{6,4},{8,10},{10,8},{12,14},{14,12},{16,18},{18,... | collective-permute-start | bytes 2654216 | tf_op jit(solution)/shard_map/ppermute | solution.py:33
  (40 other events, 422.9 us)
